TPU v7x, 32 devices: a whole 2x2x4 slice. The times are simulated.
32 devices in a mesh: seq: 8 (over z, x), head: 4 (over y, core).
Axes of the slice: x: 2, y: 2, z: 4, core: 2. Of those that a mesh axis runs over, the one named last changes fastest.
Arguments:
- queries: bfloat16 [4096, 4096], P('seq', 'head'), may hold values from -6 to 6
- keys: bfloat16 [4096, 4096], P('seq', 'head'), may hold values from -6 to 6
- values: bfloat16 [4096, 4096], P('seq', 'head'), may hold values from -6 to 6
- log_decay: float32 [32, 4096], P('head', 'seq'), may hold values from -3 to 0
- beta: float32 [32, 4096], P('head', 'seq'), may hold values from 0.001 to 0.03
- level_weights: float32 [10, 32, 4096], P(None, 'head', 'seq'), may hold values from 0.25 to 2
- doc_start: int32 [64], P('seq'), may hold values from 0 to 1, as said below
- norm_gain: float32 [4096], P('head'), may hold values from 0.25 to 1.75
- out_weight: bfloat16 [4096, 4096], P('head'), may hold values from -0.09375 to 0.09375
Outputs:
- mixed: bfloat16 [4096, 4096], P(('seq', 'head'))
Inputs may be any that keep to these rules, and one draw needn't show every extreme that they name: doc_start is 0 on the first 32 spans; the second half holds at least one 1.
All inputs are finite; a program needn't handle non-finite values.
Results may differ from a plain program's by a relative error of at most 0.014.
Values may be sent and summed in bfloat16 or wider, within the bound.
A program may use at most 128 MiB of HBM per device.

v0:
```python
import functools

import jax
import jax.numpy as jnp
from jax import lax
from jax.experimental import pallas as pl
from jax.experimental.pallas import tpu as pltpu
from jax.sharding import PartitionSpec as P

SPAN = 64
EPS = 1e-06
BF = jnp.bfloat16
F32 = jnp.float32


def mm(a, b):
    return jnp.dot(a.astype(BF), b.astype(BF), preferred_element_type=F32)


def mm_nt(a, b):
    return lax.dot_general(
        a.astype(BF), b.astype(BF), (((1,), (1,)), ((), ())), preferred_element_type=F32
    )


def mm_tn(a, b):
    return lax.dot_general(
        a.astype(BF), b.astype(BF), (((0,), (0,)), ((), ())), preferred_element_type=F32
    )


def normalize(vector):
    return vector * lax.rsqrt(jnp.sum(vector * vector, axis=-1, keepdims=True) + EPS)


def prefix_sum(rows):
    lane = lax.broadcasted_iota(jnp.int32, rows.shape, 1)
    reach = 1
    while reach < rows.shape[1]:
        rows = rows + jnp.where(lane >= reach, pltpu.roll(rows, reach, 1), 0.0)
        reach *= 2
    return rows


def document_ids(doc_ref, shape, dim):
    span = lax.broadcasted_iota(jnp.int32, shape, dim) // SPAN
    ids = jnp.zeros(shape, jnp.int32)
    for c in range(doc_ref.shape[0]):
        ids = ids + jnp.where(span >= c, doc_ref[c], 0)
    return ids


def fill_bias(doc_ref, bias_ref):
    tokens = bias_ref.shape[0]
    ids_col = document_ids(doc_ref, (tokens, 1), 0)
    ids_row = document_ids(doc_ref, (1, tokens), 1)
    rows = lax.broadcasted_iota(jnp.int32, (tokens, tokens), 0)
    cols = lax.broadcasted_iota(jnp.int32, (tokens, tokens), 1)
    valid = (rows >= cols) & (ids_col == ids_row)
    bias_ref[...] = jnp.where(valid, 0.0, -1e30)


def columns_of(rows):
    count, tokens = rows[0].shape[0] * len(rows), rows[0].shape[1]
    pad = -count % 8
    if pad:
        rows = rows + [jnp.zeros((pad, tokens), F32)]
    return jnp.concatenate(rows, axis=0).T


def unit_lower_inverse(lower):
    size = lower.shape[0]
    rows = lax.broadcasted_iota(jnp.int32, (size, size), 0)
    cols = lax.broadcasted_iota(jnp.int32, (size, size), 1)
    apart = rows ^ cols
    eye = jnp.where(apart == 0, 1.0, 0.0)
    base = 16
    power = jnp.where((apart < base) & (apart > 0), lower, 0.0)
    inverse = eye - power
    reach = 2
    while reach < base:
        power = mm(power, power)
        inverse = inverse + mm(inverse, power)
        reach *= 2
    while base < size:
        off = jnp.where((apart >= base) & (apart < 2 * base), lower, 0.0)
        inverse = inverse - mm(mm(inverse, off), inverse)
        base *= 2
    return inverse


def summary_kernel(
    heads_step, doc_ref, k_ref, v_ref, log_ref, beta_ref, map_ref, inv_ref, erase_ref, bias_ref, cum_ref
):
    tokens = k_ref.shape[0]
    half = tokens // 2
    step = pl.program_id(0)

    @pl.when(step == 0)
    def _():
        fill_bias(doc_ref, bias_ref)
        cum_ref[...] = prefix_sum(log_ref[...])

    ids_col = document_ids(doc_ref, (tokens, 1), 0)
    first = ids_col == 0
    last = ids_col == jnp.max(ids_col)
    hd = 128
    eye = jnp.where(
        lax.broadcasted_iota(jnp.int32, (hd, hd), 0) == lax.broadcasted_iota(jnp.int32, (hd, hd), 1),
        1.0,
        0.0,
    )
    for j in range(heads_step):
        h = step * heads_step + j
        cols = slice(j * hd, (j + 1) * hd)
        key = normalize(k_ref[:, cols].astype(F32))
        key_b = key.astype(BF)
        cum_row = cum_ref[pl.ds(h, 1), :]
        side = columns_of([cum_row, beta_ref[pl.ds(h, 1), :]])
        cum, beta = side[:, 0:1], side[:, 1:2]
        gamma = jnp.where(first, jnp.exp(cum), 0.0)
        total = cum_row[:, tokens - 1 : tokens]
        tail = jnp.where(last, jnp.exp(total - cum), 0.0)

        def lower(r, c):
            rs, cs = slice(r * half, (r + 1) * half), slice(c * half, (c + 1) * half)
            ratio = jnp.exp(cum[rs] - cum_row[:, cs] + bias_ref[rs, cs])
            return ratio * mm_nt(key_b[rs], key_b[cs]) * beta[rs]

        inv0 = unit_lower_inverse(lower(0, 0)).astype(BF)
        inv1 = unit_lower_inverse(lower(1, 1)).astype(BF)
        inv10 = -mm(mm(inv1, lower(1, 0)), inv0)
        inv10 = inv10.astype(BF)
        inv_ref[j, 0] = inv0
        inv_ref[j, 1] = inv10
        inv_ref[j, 2] = inv1
        rhs = jnp.concatenate(
            [beta * v_ref[:, cols].astype(F32), (beta * gamma) * key], axis=1
        ).astype(BF)
        solved0 = mm(inv0, rhs[:half])
        solved1 = mm(inv10, rhs[:half]) + mm(inv1, rhs[half:])
        solved = jnp.concatenate([solved0, solved1], axis=0).astype(BF)
        erase_ref[:, cols] = solved[:, hd:]
        out = mm_tn(tail * key, solved)
        map_ref[0, j] = (gamma[tokens - 1 : tokens, :] * eye - out[:, hd:]).astype(BF)
        map_ref[1, j] = out[:, :hd].astype(BF)


def local_kernel(
    heads_step, doc_ref, q_ref, k_ref, v_ref, log_ref, beta_ref, w_ref, inv_ref, erase_ref,
    y_ref, reader_ref, bias_ref, cum_ref,
):
    tokens = k_ref.shape[0]
    half = tokens // 2
    quarter = half // 2
    step = pl.program_id(0)

    @pl.when(step == 0)
    def _():
        fill_bias(doc_ref, bias_ref)
        cum_ref[...] = prefix_sum(log_ref[...])

    first = document_ids(doc_ref, (tokens, 1), 0) == 0
    hd = 128
    rows = lax.broadcasted_iota(jnp.int32, (quarter, quarter), 0)
    cols_i = lax.broadcasted_iota(jnp.int32, (quarter, quarter), 1)
    same_span = (rows ^ cols_i) < SPAN
    for j in range(heads_step):
        h = step * heads_step + j
        cols = slice(j * hd, (j + 1) * hd)
        key_b = normalize(k_ref[:, cols].astype(F32)).astype(BF)
        query = normalize(q_ref[:, cols].astype(F32))
        query_b = query.astype(BF)
        cum_row = cum_ref[pl.ds(h, 1), :]
        side = columns_of(
            [cum_row, beta_ref[pl.ds(h, 1), :]] + [w_ref[l, pl.ds(h, 1), :] for l in range(4)]
        )
        cum, beta = side[:, 0:1], side[:, 1:2]
        weights = [side[:, 2 + l : 3 + l] for l in range(4)]
        gamma = jnp.where(first, jnp.exp(cum), 0.0)

        def scores(r, c):
            rs, cs = slice(r * half, (r + 1) * half), slice(c * half, (c + 1) * half)
            ratio = jnp.exp(cum[rs] - cum_row[:, cs] + bias_ref[rs, cs])
            return (ratio * mm_nt(query_b[rs], key_b[cs])).astype(BF)

        def within(block, r):
            lo = r * half
            mid = lo + quarter
            a = block[:quarter, :quarter]
            a = a * jnp.where(same_span, weights[0][lo:mid], weights[1][lo:mid])
            b = block[quarter:, :quarter] * weights[2][mid : mid + quarter]
            c = block[quarter:, quarter:]
            c = c * jnp.where(
                same_span, weights[0][mid : mid + quarter], weights[1][mid : mid + quarter]
            )
            top = jnp.concatenate([a, jnp.zeros_like(a)], axis=1)
            return jnp.concatenate([top, jnp.concatenate([b, c], axis=1)], axis=0)

        s00, s10, s11 = scores(0, 0), scores(1, 0), scores(1, 1)
        inv0, inv10, inv1 = inv_ref[j, 0], inv_ref[j, 1], inv_ref[j, 2]
        r00 = within(mm(s00, inv0), 0)
        r11 = within(mm(s11, inv1), 1)
        r10 = (mm(s10, inv0) + mm(s11, inv10)) * weights[3][half:]
        value = (beta * v_ref[:, cols].astype(F32)).astype(BF)
        y_ref[:half, cols] = mm(r00, value[:half])
        y_ref[half:, cols] = mm(r10, value[:half]) + mm(r11, value[half:])
        erase = erase_ref[:, cols]
        reader_ref[:half, cols] = (gamma[:half] * query[:half] - mm(s00, erase[:half])).astype(BF)
        reader_ref[half:, cols] = (
            gamma[half:] * query[half:] - mm(s10, erase[:half]) - mm(s11, erase[half:])
        ).astype(BF)


def finish_kernel(heads_step, low, y_ref, reader_ref, state_ref, w_ref, gain_ref, z_ref):
    step = pl.program_id(0)
    hd = 128
    levels = state_ref.shape[0]
    for j in range(heads_step):
        h = step * heads_step + j
        cols = slice(j * hd, (j + 1) * hd)
        side = columns_of([w_ref[low + l, pl.ds(h, 1), :] for l in range(levels)])
        y = y_ref[:, cols]
        reader = reader_ref[:, cols]
        for l in range(levels):
            y = y + side[:, l : l + 1] * mm(reader, state_ref[l, j])
        y = y * lax.rsqrt(jnp.mean(y * y, axis=-1, keepdims=True) + EPS)
        z_ref[:, cols] = (y * gain_ref[:, cols]).astype(BF)


def from_partner(value, axis, distance):
    return lax.ppermute(value, axis, [(i, i ^ 1 << distance) for i in range(lax.axis_size(axis))])


def bmm(a, b):
    return jnp.einsum("hde,hef->hdf", a, b, preferred_element_type=F32)


def body(queries, keys, values, log_decay, beta, level_weights, doc_start, norm_gain, out_weight):
    tokens = queries.shape[0]
    heads = log_decay.shape[0]
    hd = queries.shape[1] // heads
    half = tokens // 2
    hs = 2
    low = (tokens // SPAN).bit_length()
    grid = (heads // hs,)
    smem = pl.BlockSpec(memory_space=pltpu.SMEM)
    wide = pl.BlockSpec((tokens, hs * hd), lambda i: (0, i))
    whole = pl.BlockSpec((heads, tokens), lambda i: (0, 0))
    level_block = pl.BlockSpec(level_weights.shape, lambda i: (0, 0, 0))
    inv_block = pl.BlockSpec((hs, 3, half, half), lambda i: (i, 0, 0, 0))
    map_block = pl.BlockSpec((2, hs, hd, hd), lambda i: (0, i, 0, 0))
    params = pltpu.CompilerParams(vmem_limit_bytes=48 * 2**20)
    scratch = [pltpu.VMEM((tokens, tokens), F32), pltpu.VMEM((heads, tokens), F32)]
    maps, inv, erase = pl.pallas_call(
        functools.partial(summary_kernel, hs),
        grid=grid,
        out_shape=(
            jax.ShapeDtypeStruct((2, heads, hd, hd), BF),
            jax.ShapeDtypeStruct((heads, 3, half, half), BF),
            jax.ShapeDtypeStruct((tokens, heads * hd), BF),
        ),
        in_specs=[smem, wide, wide, whole, whole],
        out_specs=(map_block, inv_block, wide),
        scratch_shapes=scratch,
        compiler_params=params,
        name="summary",
    )(doc_start, keys, values, log_decay, beta)

    y_local, reader = pl.pallas_call(
        functools.partial(local_kernel, hs),
        grid=grid,
        out_shape=(
            jax.ShapeDtypeStruct((tokens, heads * hd), F32),
            jax.ShapeDtypeStruct((tokens, heads * hd), BF),
        ),
        in_specs=[smem, wide, wide, wide, whole, whole, level_block, inv_block, wide],
        out_specs=(wide, wide),
        scratch_shapes=scratch,
        compiler_params=params,
        cost_estimate=pl.CostEstimate(flops=4 * 10**9, bytes_accessed=12 * 10**6, transcendentals=0),
        name="local",
    )(doc_start, queries, keys, values, log_decay, beta, level_weights, inv, erase)

    nbits = lax.axis_size("seq").bit_length() - 1
    block_idx = lax.axis_index("seq")
    current = maps
    carried = None
    states = []
    for bit in range(nbits):
        sibling = from_partner(current, "seq", bit)
        upper = block_idx >> bit & 1 == 1
        if carried is None:
            reached = sibling.astype(F32)
        else:
            both = jnp.concatenate([sibling[0], sibling[1]], axis=-1)
            reached = bmm(carried.astype(BF), both)
            reached = jnp.stack([reached[..., :hd], reached[..., hd:]])
        states.append(jnp.where(upper, reached[1], 0.0).astype(BF))
        if bit < nbits - 1:
            idle = jnp.broadcast_to(jnp.eye(hd, dtype=F32), (heads, hd, hd)) if bit == 0 else carried
            carried = jnp.where(upper, reached[0], idle)
            first = jnp.where(upper, sibling, current)
            second = jnp.where(upper, current, sibling)
            both = jnp.concatenate([first[0], first[1]], axis=-1)
            merged = bmm(second[0], both)
            current = jnp.stack(
                [merged[..., :hd], merged[..., hd:] + second[1].astype(F32)]
            ).astype(BF)
    states = jnp.stack(states)

    normed = pl.pallas_call(
        functools.partial(finish_kernel, hs, low),
        grid=grid,
        out_shape=jax.ShapeDtypeStruct((tokens, heads * hd), BF),
        in_specs=[
            wide,
            wide,
            pl.BlockSpec((nbits, hs, hd, hd), lambda i: (0, i, 0, 0)),
            level_block,
            pl.BlockSpec((1, hs * hd), lambda i: (0, i)),
        ],
        out_specs=wide,
        compiler_params=params,
        name="finish",
    )(y_local, reader, states, level_weights, norm_gain.reshape(1, -1))
    return lax.psum_scatter(
        jnp.dot(normed, out_weight, preferred_element_type=F32).astype(BF),
        "head",
        scatter_dimension=0,
        tiled=True,
    )


def solution(mesh):
    placed = (
        P("seq", "head"),
        P("seq", "head"),
        P("seq", "head"),
        P("head", "seq"),
        P("head", "seq"),
        P(None, "head", "seq"),
        P("seq"),
        P("head"),
        P("head", None),
    )
    return jax.shard_map(
        body, mesh=mesh, in_specs=placed, out_specs=P(("seq", "head"), None), check_vma=False
    )
```

profile of v0, /device:TPU:0, one launch (start us, length us, event | category | flops | bytes accessed | tf_op | source)
XLA Modules:
  0.0 167.0 jit_solution(15639992222620362830)
XLA Ops:
  6.5 1.2 copy-done.1
  7.8 1.2 copy-done.3
  9.0 0.7 copy-done.6
  9.7 0.7 copy-done.8
  10.4 0.7 copy-done.11
  11.1 36.5 %summary.1 = (bf16[2,8,128,128]{3,2,1,0:T(8,128)(2,1)S(1)}, bf16[8,3,256,256]{3,2,1,0:T(8,128)(2,1)}, bf16[512,1024]{1,0:T(8,128)(2,1)S(1)}) custom-call(s32[8]{0:T(128)S(1)} %copy-done.11, bf16[512,1024]{1,0:T(8,128)(2,1)S(1)} %copy-done.1, bf16[512,1024]{1,0:T(8,128)(2,1)S(1)} %copy-done.3, f32[8,512]{1,0:T(8,128)S(1)} %copy-done.6, f32[8,512]{1,0:T(8,128)S(1)} %copy-done.8), custom_call_target="tpu_custom_call" | custom-call | tf_op jit(solution)/shard_map/summary/pallas_call | solution.py:255
  47.6 1.0 copy-done.14
  48.6 2.9 %collective-permute-start = (bf16[2,8,128,128]{3,2,1,0:T(8,128)(2,1)S(1)}, bf16[2,8,128,128]{3,2,1,0:T(8,128)(2,1)S(1)}, u32[]{:S(2)}, u32[]{:S(2)}) collective-permute-start(bf16[2,8,128,128]{3,2,1,0:T(8,128)(2,1)S(1)} %get-tuple-element.14), channel_id=1, source_target_pairs={{0,4},{4,0},{8,12},{12,8},{16,20},{20,16},{24,28},{28,24},{1,5},{5... | collective-permute-start | bytes 1572872 | tf_op jit(solution)/shard_map/ppermute | solution.py:232
  51.5 11.9 %collective-permute-done = bf16[2,8,128,128]{3,2,1,0:T(8,128)(2,1)S(1)} collective-permute-done((bf16[2,8,128,128]{3,2,1,0:T(8,128)(2,1)S(1)}, bf16[2,8,128,128]{3,2,1,0:T(8,128)(2,1)S(1)}, u32[]{:S(2)}, u32[]{:S(2)}) %collective-permute-start) | collective-permute-done | bytes 524320 | tf_op jit(solution)/shard_map/ppermute | solution.py:232
  63.4 0.1 broadcast_select_fusion.3
  63.6 0.3 fusion.8
  63.9 0.1 fusion.23
  64.0 0.1 pad_maximum_fusion.1
  64.1 1.9 %collective-permute-start.1 = (bf16[2,8,128,128]{3,2,1,0:T(8,128)(2,1)S(1)}, bf16[2,8,128,128]{3,2,1,0:T(8,128)(2,1)S(1)}, u32[]{:S(2)}, u32[]{:S(2)}) collective-permute-start(bf16[2,8,128,128]{3,2,1,0:T(8,128)(2,1)S(1)} %pad_maximum_fusion.1), channel_id=1, source_target_pairs={{0,8},{4,12},{8,0},{12,4},{16,24},{20,28},{24,16},{28,20},{1,9},{5... | collective-permute-start | bytes 1572872 | tf_op jit(solution)/shard_map/ppermute | solution.py:232
  66.0 1.2 copy-done.13
  67.2 1.2 copy-done.15
  68.5 10.1 %local.1 = (f32[512,1024]{1,0:T(8,128)}, bf16[512,1024]{1,0:T(8,128)(2,1)S(1)}) custom-call(s32[8]{0:T(128)S(1)} %copy-done.12, bf16[512,1024]{1,0:T(8,128)(2,1)S(1)} %copy-done.13, bf16[512,1024]{1,0:T(8,128)(2,1)S(1)} %copy-done.2, bf16[512,1024]{1,0:T(8,128)(2,1)S(1)} %copy-done.4, f32[8,512]{1,0:T(8,128)S(1)} %copy-done.7, f32[8,512]{1,0:T(8,128)S(1)} %copy-done.9, ...), custom_call_target="tpu_custom_call" | custom-call | flops 4000000000 | bytes 12000000 | tf_op jit(solution)/shard_map/local/pallas_call | solution.py:270
  78.6 0.1 fusion.7
  78.7 0.1 broadcast_select_fusion.1
  78.8 0.3 fusion.16
  79.1 0.1 fusion.27
  79.2 0.1 pad_maximum_fusion.2
  79.3 2.6 %collective-permute-start.2 = (bf16[2,8,128,128]{3,2,1,0:T(8,128)(2,1)S(1)}, bf16[2,8,128,128]{3,2,1,0:T(8,128)(2,1)S(1)}, u32[]{:S(2)}, u32[]{:S(2)}) collective-permute-start(bf16[2,8,128,128]{3,2,1,0:T(8,128)(2,1)S(1)} %pad_maximum_fusion.2), channel_id=1, source_target_pairs={{0,16},{4,20},{8,24},{12,28},{16,0},{20,4},{24,8},{28,12},{1,17},{... | collective-permute-start | bytes 1572872 | tf_op jit(solution)/shard_map/ppermute | solution.py:232
  82.0 0.3 fusion.12
  82.3 0.1 fusion.24
  82.4 21.6 %collective-permute-done.2 = bf16[2,8,128,128]{3,2,1,0:T(8,128)(2,1)S(1)} collective-permute-done((bf16[2,8,128,128]{3,2,1,0:T(8,128)(2,1)S(1)}, bf16[2,8,128,128]{3,2,1,0:T(8,128)(2,1)S(1)}, u32[]{:S(2)}, u32[]{:S(2)}) %collective-permute-start.2) | collective-permute-done | bytes 524320 | tf_op jit(solution)/shard_map/ppermute | solution.py:232
  104.0 0.2 fusion.1
  104.2 0.1 pad_maximum_fusion.state_ref
  104.4 4.7 %finish.1 = bf16[512,1024]{1,0:T(8,128)(2,1)S(1)} custom-call(f32[512,1024]{1,0:T(8,128)S(1)} %copy-done, bf16[512,1024]{1,0:T(8,128)(2,1)S(1)} %get-tuple-element.13.reader_ref, bf16[3,8,128,128]{3,2,1,0:T(8,128)(2,1)S(1)} %pad_maximum_fusion.state_ref, f32[10,8,512]{2,1,0:T(8,128)S(1)} %copy-done.5, f32[1,1024]{1,0:T(1,128)S(1)} %bitcast.57), custom_call_target="tpu_custom_call" | custom-call | tf_op jit(solution)/shard_map/finish/pallas_call | solution.py:312
  109.1 6.2 %convolution_convert_fusion = bf16[512,4096]{1,0:T(8,128)(2,1)} fusion(bf16[512,1024]{1,0:T(8,128)(2,1)S(1)} %finish.1, bf16[1024,4096]{1,0:T(8,128)(2,1)S(1)} %bitcast.59), kind=kOutput, calls=%fused_computation | convolution fusion | flops 4297064448 | bytes 13631488 | tf_op jit(solution)/shard_map/dot_general | solution.py:328
  115.3 0.0 reduce-scatter.2.cloned.1.call-update
  115.3 44.8 %reduce-scatter.2.cloned.1.call-done = bf16[128,4096]{1,0:T(8,128)(2,1)} async-done(((bf16[512,4096]{1,0:T(8,128)(2,1)}), bf16[128,4096]{1,0:T(8,128)(2,1)}) %reduce-scatter.2.cloned.1.call-update) | async-done | bytes 1048592 | tf_op jit(solution)/shard_map/reduce_scatter | solution.py:327
  (38 shorter events, 0.3 us)
Async XLA Ops:
  6.5 153.6 %reduce-scatter.2.cloned.1.call-start = ((), (), s32[]{:S(2)}) async-start(), calls=%async_computation.1 | async-start | bytes 5242880 | tf_op jit(solution)/shard_map/reduce_scatter | solution.py:327
  6.5 1.2 copy-start.1
  7.8 1.2 copy-start.3
  9.0 0.7 copy-start.6
  9.7 0.7 copy-start.8
  10.4 0.7 copy-start.11
  11.1 54.9 %copy-start.2 = (bf16[512,1024]{1,0:T(8,128)(2,1)S(1)}, bf16[512,1024]{1,0:T(8,128)(2,1)}, u32[]{:S(2)}) copy-start(bf16[512,1024]{1,0:T(8,128)(2,1)} %k_ref.3) | copy-start | bytes 3145732
  11.1 54.9 %copy-start.4 = (bf16[512,1024]{1,0:T(8,128)(2,1)S(1)}, bf16[512,1024]{1,0:T(8,128)(2,1)}, u32[]{:S(2)}) copy-start(bf16[512,1024]{1,0:T(8,128)(2,1)} %v_ref.3) | copy-start | bytes 3145732
  11.1 54.9 %copy-start.5 = (f32[10,8,512]{2,1,0:T(8,128)S(1)}, f32[10,8,512]{2,1,0:T(8,128)}, u32[]{:S(2)}) copy-start(f32[10,8,512]{2,1,0:T(8,128)} %w_ref.3) | copy-start | bytes 491524
  11.1 54.9 %copy-start.7 = (f32[8,512]{1,0:T(8,128)S(1)}, f32[8,512]{1,0:T(8,128)}, u32[]{:S(2)}) copy-start(f32[8,512]{1,0:T(8,128)} %log_ref.3) | copy-start | bytes 49156
  11.1 54.9 %copy-start.9 = (f32[8,512]{1,0:T(8,128)S(1)}, f32[8,512]{1,0:T(8,128)}, u32[]{:S(2)}) copy-start(f32[8,512]{1,0:T(8,128)} %beta_ref.3) | copy-start | bytes 49156
  11.1 54.9 %copy-start.12 = (s32[8]{0:T(128)S(1)}, s32[8]{0:T(128)}, u32[]{:S(2)}) copy-start(s32[8]{0:T(128)} %doc_ref.3) | copy-start | bytes 100
  47.6 1.0 copy-start.14
  48.6 14.9 %collective-permute-start = (bf16[2,8,128,128]{3,2,1,0:T(8,128)(2,1)S(1)}, bf16[2,8,128,128]{3,2,1,0:T(8,128)(2,1)S(1)}, u32[]{:S(2)}, u32[]{:S(2)}) collective-permute-start(bf16[2,8,128,128]{3,2,1,0:T(8,128)(2,1)S(1)} %get-tuple-element.14), channel_id=1, source_target_pairs={{0,4},{4,0},{8,12},{12,8},{16,20},{20,16},{24,28},{28,24},{1,5},{5... | collective-permute-start | bytes 1572872 | tf_op jit(solution)/shard_map/ppermute | solution.py:232
  64.1 14.6 %collective-permute-start.1 = (bf16[2,8,128,128]{3,2,1,0:T(8,128)(2,1)S(1)}, bf16[2,8,128,128]{3,2,1,0:T(8,128)(2,1)S(1)}, u32[]{:S(2)}, u32[]{:S(2)}) collective-permute-start(bf16[2,8,128,128]{3,2,1,0:T(8,128)(2,1)S(1)} %pad_maximum_fusion.1), channel_id=1, source_target_pairs={{0,8},{4,12},{8,0},{12,4},{16,24},{20,28},{24,16},{28,20},{1,9},{5... | collective-permute-start | bytes 1572872 | tf_op jit(solution)/shard_map/ppermute | solution.py:232
  66.0 1.2 copy-start.13
  67.2 1.2 copy-start.15
  78.6 25.7 %copy-start = (f32[512,1024]{1,0:T(8,128)S(1)}, f32[512,1024]{1,0:T(8,128)}, u32[]{:S(2)}) copy-start(f32[512,1024]{1,0:T(8,128)} %get-tuple-element.12.y_ref) | copy-start | bytes 6291460
  78.6 25.7 %copy-start.10 = (f32[1024]{0:T(1024)S(1)}, f32[1024]{0:T(1024)}, u32[]{:S(2)}) copy-start(f32[1024]{0:T(1024)} %param.16) | copy-start | bytes 12292
  78.8 30.3 %slice-start = ((s8[8388608]{0:T(1024)(128)(4,1)}), s8[4194304]{0:T(1024)(128)(4,1)S(1)}, s32[]{:S(2)}) async-start(s8[8388608]{0:T(1024)(128)(4,1)} %bitcast.58), calls=%async_computation.2 | async-start | bytes 8388608
  79.3 24.7 %collective-permute-start.2 = (bf16[2,8,128,128]{3,2,1,0:T(8,128)(2,1)S(1)}, bf16[2,8,128,128]{3,2,1,0:T(8,128)(2,1)S(1)}, u32[]{:S(2)}, u32[]{:S(2)}) collective-permute-start(bf16[2,8,128,128]{3,2,1,0:T(8,128)(2,1)S(1)} %pad_maximum_fusion.2), channel_id=1, source_target_pairs={{0,16},{4,20},{8,24},{12,28},{16,0},{20,4},{24,8},{28,12},{1,17},{... | collective-permute-start | bytes 1572872 | tf_op jit(solution)/shard_map/ppermute | solution.py:232
  82.3 26.8 %slice-start.1 = ((s8[8388608]{0:T(1024)(128)(4,1)}), s8[4194304]{0:T(1024)(128)(4,1)S(1)}, s32[]{:S(2)}) async-start(s8[8388608]{0:T(1024)(128)(4,1)} %bitcast.58), calls=%async_computation.3 | async-start | bytes 8388608
Sparse Core Ops, SparseCore 0:
  115.4 44.6 reduce-scatter.1
where the time goes:
time: 167 us
  waiting for transfers between devices  78.3 us (47%)
  Pallas kernels  51.4 us (31%)
  between operations  13.7 us (8%)
  local copies, waits for them, and re-layouts  8.23 us (5%)
  starting transfers between devices  7.48 us (4%)
  matrix products  7.27 us (4%)
    reduce_scatter x1, waiting for transfers between devices, body(): lax.psum_scatter(jnp.dot(normed, out_weight, preferred_element_type=F32)....  44.8 us
    pallas_call x1, Pallas kernels, body(): pl.pallas_call(functools.partial(summary_kernel, hs), grid=grid, out_shap...  36.5 us
    ppermute x3, waiting for transfers between devices, from_partner(): lax.ppermute(value, axis, [(i, i ^ 1 << distance) for i in range(lax.axis...  33.5 us
    pallas_call x1, Pallas kernels, body(): pl.pallas_call(functools.partial(local_kernel, hs), grid=grid, out_shape=...  10.1 us
    unnamed x36, local copies, waits for them, and re-layouts  8 us
    ppermute x3, starting transfers between devices, from_partner(): lax.ppermute(value, axis, [(i, i ^ 1 << distance) for i in range(lax.axis...  7.48 us
    dot_general x1, matrix products, body(): jnp.dot(normed, out_weight, preferred_element_type=F32).astype(BF)  6.17 us
    pallas_call x1, Pallas kernels, body(): pl.pallas_call(functools.partial(finish_kernel, hs, low), grid=grid, out_...  4.73 us
  transfers between devices with their start and end apart: 4, of which 3 were waited for; matrix products, arithmetic and copies ran while one was open for 0% of the time, Pallas kernels for 6%

commit v1 on v0

--- a/solution.py
+++ b/solution.py
@@ -68,25 +68,38 @@
     return jnp.concatenate(rows, axis=0).T
 
 
-def unit_lower_inverse(lower):
-    size = lower.shape[0]
+def unit_lower_inverses(lowers):
+    size = lowers[0].shape[0]
     rows = lax.broadcasted_iota(jnp.int32, (size, size), 0)
     cols = lax.broadcasted_iota(jnp.int32, (size, size), 1)
     apart = rows ^ cols
     eye = jnp.where(apart == 0, 1.0, 0.0)
     base = 16
-    power = jnp.where((apart < base) & (apart > 0), lower, 0.0)
-    inverse = eye - power
+    inside = (apart < base) & (apart > 0)
+    powers = [jnp.where(inside, lower, 0.0) for lower in lowers]
+    inverses = [eye - power for power in powers]
+    powers = [mm(power, power) for power in powers]
     reach = 2
     while reach < base:
-        power = mm(power, power)
-        inverse = inverse + mm(inverse, power)
+        if 2 * reach < base:
+            both = [
+                mm(jnp.concatenate([power.astype(BF), inverse.astype(BF)], axis=0), power)
+                for power, inverse in zip(powers, inverses)
+            ]
+            powers = [pair[:size] for pair in both]
+            inverses = [inverse + pair[size:] for inverse, pair in zip(inverses, both)]
+        else:
+            inverses = [inverse + mm(inverse, power) for power, inverse in zip(powers, inverses)]
         reach *= 2
     while base < size:
-        off = jnp.where((apart >= base) & (apart < 2 * base), lower, 0.0)
-        inverse = inverse - mm(mm(inverse, off), inverse)
+        band = (apart >= base) & (apart < 2 * base)
+        offs = [jnp.where(band, lower, 0.0).astype(BF) for lower in lowers]
+        held = [inverse.astype(BF) for inverse in inverses]
+        steps = [mm(inverse, off) for inverse, off in zip(held, offs)]
+        steps = [mm(first, inverse) for first, inverse in zip(steps, held)]
+        inverses = [inverse - step for inverse, step in zip(inverses, steps)]
         base *= 2
-    return inverse
+    return [inverse.astype(BF) for inverse in inverses]
 
 
 def summary_kernel(
@@ -102,45 +115,64 @@
         cum_ref[...] = prefix_sum(log_ref[...])
 
     ids_col = document_ids(doc_ref, (tokens, 1), 0)
-    first = ids_col == 0
-    last = ids_col == jnp.max(ids_col)
+    first_doc = ids_col == 0
+    last_doc = ids_col == jnp.max(ids_col)
     hd = 128
     eye = jnp.where(
         lax.broadcasted_iota(jnp.int32, (hd, hd), 0) == lax.broadcasted_iota(jnp.int32, (hd, hd), 1),
         1.0,
         0.0,
     )
-    for j in range(heads_step):
-        h = step * heads_step + j
-        cols = slice(j * hd, (j + 1) * hd)
-        key = normalize(k_ref[:, cols].astype(F32))
-        key_b = key.astype(BF)
-        cum_row = cum_ref[pl.ds(h, 1), :]
-        side = columns_of([cum_row, beta_ref[pl.ds(h, 1), :]])
-        cum, beta = side[:, 0:1], side[:, 1:2]
-        gamma = jnp.where(first, jnp.exp(cum), 0.0)
-        total = cum_row[:, tokens - 1 : tokens]
-        tail = jnp.where(last, jnp.exp(total - cum), 0.0)
-
-        def lower(r, c):
-            rs, cs = slice(r * half, (r + 1) * half), slice(c * half, (c + 1) * half)
-            ratio = jnp.exp(cum[rs] - cum_row[:, cs] + bias_ref[rs, cs])
-            return ratio * mm_nt(key_b[rs], key_b[cs]) * beta[rs]
-
-        inv0 = unit_lower_inverse(lower(0, 0)).astype(BF)
-        inv1 = unit_lower_inverse(lower(1, 1)).astype(BF)
-        inv10 = -mm(mm(inv1, lower(1, 0)), inv0)
-        inv10 = inv10.astype(BF)
+    heads = range(heads_step)
+    col_of = [slice(j * hd, (j + 1) * hd) for j in heads]
+    keys = [normalize(k_ref[:, c].astype(F32)) for c in col_of]
+    keys_b = [key.astype(BF) for key in keys]
+    cum_rows = [cum_ref[pl.ds(step * heads_step + j, 1), :] for j in heads]
+    sides = [
+        columns_of([cum_rows[j], beta_ref[pl.ds(step * heads_step + j, 1), :]]) for j in heads
+    ]
+    cums, betas = [side[:, 0:1] for side in sides], [side[:, 1:2] for side in sides]
+    quarter = half // 2
+    parts = tokens // quarter
+
+    def lower(j, rs, cs):
+        ratio = jnp.exp(cums[j][rs] - cum_rows[j][:, cs] + bias_ref[rs, cs])
+        return ratio * mm_nt(keys_b[j][rs], keys_b[j][cs]) * betas[j][rs]
+
+    piece = [slice(i * quarter, (i + 1) * quarter) for i in range(parts)]
+    diagonal = unit_lower_inverses([lower(j, p, p) for j in heads for p in piece])
+    merges = [(j, i) for j in heads for i in range(0, parts, 2)]
+    firsts = [
+        mm(diagonal[j * parts + i + 1], lower(j, piece[i + 1], piece[i])) for j, i in merges
+    ]
+    corners = [
+        -mm(first, diagonal[j * parts + i]) for first, (j, i) in zip(firsts, merges)
+    ]
+    inverses = []
+    for corner, (j, i) in zip(corners, merges):
+        a, b = diagonal[j * parts + i], diagonal[j * parts + i + 1]
+        top = jnp.concatenate([a, jnp.zeros_like(a)], axis=1)
+        inverses.append(
+            jnp.concatenate([top, jnp.concatenate([corner.astype(BF), b], axis=1)], axis=0)
+        )
+    low, high = slice(0, half), slice(half, tokens)
+    firsts = [mm(inverses[2 * j + 1], lower(j, high, low)) for j in heads]
+    cross = [(-mm(first, inverses[2 * j])).astype(BF) for j, first in enumerate(firsts)]
+    for j in heads:
+        c, key, cum, beta = col_of[j], keys[j], cums[j], betas[j]
+        inv0, inv10, inv1 = inverses[2 * j], cross[j], inverses[2 * j + 1]
         inv_ref[j, 0] = inv0
         inv_ref[j, 1] = inv10
         inv_ref[j, 2] = inv1
+        gamma = jnp.where(first_doc, jnp.exp(cum), 0.0)
+        tail = jnp.where(last_doc, jnp.exp(cum_rows[j][:, tokens - 1 : tokens] - cum), 0.0)
         rhs = jnp.concatenate(
-            [beta * v_ref[:, cols].astype(F32), (beta * gamma) * key], axis=1
+            [beta * v_ref[:, c].astype(F32), (beta * gamma) * key], axis=1
         ).astype(BF)
         solved0 = mm(inv0, rhs[:half])
         solved1 = mm(inv10, rhs[:half]) + mm(inv1, rhs[half:])
         solved = jnp.concatenate([solved0, solved1], axis=0).astype(BF)
-        erase_ref[:, cols] = solved[:, hd:]
+        erase_ref[:, c] = solved[:, hd:]
         out = mm_tn(tail * key, solved)
         map_ref[0, j] = (gamma[tokens - 1 : tokens, :] * eye - out[:, hd:]).astype(BF)
         map_ref[1, j] = out[:, :hd].astype(BF)
@@ -228,6 +260,122 @@
         z_ref[:, cols] = (y * gain_ref[:, cols]).astype(BF)
 
 
+def project_kernel(
+    chunk, z_ref, w_hbm, out_ref, w_ref, keep, send_a, recv_a, send_y, recv_y, send_b, recv_b,
+    w_sem, sa_sem, ra_sem, sy_sem, ry_sem, sb_sem, rb_sem,
+):
+    me = lax.axis_index("head")
+    mate = me + 1 - 2 * (me % 2)
+    across = (me + 2) % 4
+    far_mate = (mate + 2) % 4
+    count = keep.shape[1]
+    rows = keep.shape[2]
+
+    def columns(j):
+        return pl.ds(pl.multiple_of(j * chunk, chunk), chunk)
+
+    def load(j):
+        return pltpu.make_async_copy(w_hbm.at[:, columns(j)], w_ref.at[:, columns(j)], w_sem.at[j])
+
+    def remote(src, dst, ssem, rsem, j, target):
+        return pltpu.make_async_remote_copy(
+            src_ref=src.at[j],
+            dst_ref=dst.at[j],
+            send_sem=ssem.at[j],
+            recv_sem=rsem.at[j],
+            device_id={"head": target},
+            device_id_type=pl.DeviceIdType.MESH,
+        )
+
+    def copy_a(j):
+        return remote(send_a, recv_a, sa_sem, ra_sem, j, mate)
+
+    def copy_b(j):
+        return remote(send_b, recv_b, sb_sem, rb_sem, j, mate)
+
+    def copy_y(j):
+        return remote(send_y, recv_y, sy_sem, ry_sem, j, across)
+
+    def block(owner):
+        return z_ref[pl.ds(pl.multiple_of(owner * rows, rows), rows), :]
+
+    lax.fori_loop(0, count, lambda j, _: (load(j).start(), 0)[1], 0)
+    barrier = pltpu.get_barrier_semaphore()
+    for other in (mate, across):
+        pl.semaphore_signal(
+            barrier, inc=1, device_id={"head": other}, device_id_type=pl.DeviceIdType.MESH
+        )
+    pl.semaphore_wait(barrier, 2)
+
+    def forward(j):
+        copy_a(j).wait_recv()
+        send_y[j] = (keep[0, j] + recv_a[j].astype(F32)).astype(BF)
+        copy_y(j).start()
+
+    def far(j, _):
+        load(j).wait()
+        weight = w_ref[:, columns(j)]
+        send_a[j] = jnp.dot(block(far_mate), weight, preferred_element_type=F32).astype(BF)
+        copy_a(j).start()
+        keep[0, j] = jnp.dot(block(across), weight, preferred_element_type=F32)
+
+        @pl.when(j > 0)
+        def _():
+            forward(j - 1)
+
+        return 0
+
+    lax.fori_loop(0, count, far, 0)
+    forward(count - 1)
+
+    def near(j, _):
+        weight = w_ref[:, columns(j)]
+        send_b[j] = jnp.dot(block(mate), weight, preferred_element_type=F32).astype(BF)
+        copy_b(j).start()
+        keep[1, j] = jnp.dot(block(me), weight, preferred_element_type=F32)
+        return 0
+
+    lax.fori_loop(0, count, near, 0)
+
+    def close(j, _):
+        copy_b(j).wait_recv()
+        copy_y(j).wait_recv()
+        total = keep[1, j] + recv_b[j].astype(F32) + recv_y[j].astype(F32)
+        out_ref[:, columns(j)] = total.astype(BF)
+        copy_a(j).wait_send()
+        copy_b(j).wait_send()
+        copy_y(j).wait_send()
+        return 0
+
+    lax.fori_loop(0, count, close, 0)
+
+
+def project(normed, out_weight):
+    tokens, width = normed.shape
+    out_width = out_weight.shape[1]
+    rows = tokens // 4
+    chunk = min(512, out_width)
+    count = out_width // chunk
+    slab = pltpu.VMEM((count, rows, chunk), BF)
+    sems = [pltpu.SemaphoreType.DMA((count,))] * 7
+    return pl.pallas_call(
+        functools.partial(project_kernel, chunk),
+        out_shape=jax.ShapeDtypeStruct((rows, out_width), BF),
+        in_specs=[pl.BlockSpec(memory_space=pltpu.VMEM), pl.BlockSpec(memory_space=pl.ANY)],
+        out_specs=pl.BlockSpec(memory_space=pltpu.VMEM),
+        scratch_shapes=[
+            pltpu.VMEM((width, out_width), BF),
+            pltpu.VMEM((2, count, rows, chunk), F32),
+        ]
+        + [slab] * 6
+        + sems,
+        compiler_params=pltpu.CompilerParams(
+            collective_id=0, has_side_effects=True, vmem_limit_bytes=56 * 2**20
+        ),
+        name="project",
+    )(normed, out_weight)
+
+
 def from_partner(value, axis, distance):
     return lax.ppermute(value, axis, [(i, i ^ 1 << distance) for i in range(lax.axis_size(axis))])
 
@@ -250,7 +398,7 @@
     level_block = pl.BlockSpec(level_weights.shape, lambda i: (0, 0, 0))
     inv_block = pl.BlockSpec((hs, 3, half, half), lambda i: (i, 0, 0, 0))
     map_block = pl.BlockSpec((2, hs, hd, hd), lambda i: (0, i, 0, 0))
-    params = pltpu.CompilerParams(vmem_limit_bytes=48 * 2**20)
+    params = pltpu.CompilerParams(vmem_limit_bytes=56 * 2**20)
     scratch = [pltpu.VMEM((tokens, tokens), F32), pltpu.VMEM((heads, tokens), F32)]
     maps, inv, erase = pl.pallas_call(
         functools.partial(summary_kernel, hs),
@@ -324,12 +472,7 @@
         compiler_params=params,
         name="finish",
     )(y_local, reader, states, level_weights, norm_gain.reshape(1, -1))
-    return lax.psum_scatter(
-        jnp.dot(normed, out_weight, preferred_element_type=F32).astype(BF),
-        "head",
-        scatter_dimension=0,
-        tiled=True,
-    )
+    return project(normed, out_weight)
 
 
 def solution(mesh):

time: 167 us -> 114 us (0.68)
  waiting for transfers between devices: 78.3 us -> 34.1 us
  Pallas kernels: 51.4 us -> 66 us
  between operations: 13.7 us -> 0.13 us
  matrix products: 7.27 us -> 1.08 us
  local copies, waits for them, and re-layouts: 8.23 us -> 2.53 us
  other arithmetic: 0.65 us -> 2.52 us
    reduce_scatter x1 -> x0, waiting for transfers between devices: 44.8 us -> none  [body(): lax.psum_scatter(jnp.dot(normed, out_weight, preferred_element_type=F32)....]
    pallas_call x0 -> x1, Pallas kernels: none -> 30.2 us  [project(): pl.pallas_call(functools.partial(project_kernel, chunk), out_shape=jax.Sh...]
    pallas_call x1, Pallas kernels: 36.5 us -> 18.7 us  [body(): pl.pallas_call(functools.partial(summary_kernel, hs), grid=grid, out_shap...]
    dot_general x1 -> x0, matrix products: 6.17 us -> none  [body(): jnp.dot(normed, out_weight, preferred_element_type=F32).astype(BF)]
    unnamed x36 -> x1, local copies, waits for them, and re-layouts: 8 us -> 2.29 us
    pallas_call x1, Pallas kernels: 4.73 us -> 6.49 us  [body(): pl.pallas_call(functools.partial(finish_kernel, hs, low), grid=grid, out_...]
  transfers between devices with their start and end apart: 4 -> 3, of which waited for: 3 -> 3; matrix products, arithmetic and copies ran while one was open for 0% -> 0% of each run, Pallas kernels for 6% -> 9%
where the time goes in v1:
time: 114 us
  Pallas kernels  66 us (58%)
  waiting for transfers between devices  34.1 us (30%)
  starting transfers between devices  7.41 us (6%)
  local copies, waits for them, and re-layouts  2.53 us (2%)
  other arithmetic  2.52 us (2%)
    ppermute x3, waiting for transfers between devices, from_partner(): lax.ppermute(value, axis, [(i, i ^ 1 << distance) for i in range(lax.axis...  34.1 us
    pallas_call x1, Pallas kernels, project(): pl.pallas_call(functools.partial(project_kernel, chunk), out_shape=jax.Sh...  30.2 us
    pallas_call x1, Pallas kernels, body(): pl.pallas_call(functools.partial(summary_kernel, hs), grid=grid, out_shap...  18.7 us
    pallas_call x1, Pallas kernels, body(): pl.pallas_call(functools.partial(local_kernel, hs), grid=grid, out_shape=...  10.6 us
    ppermute x3, starting transfers between devices, from_partner(): lax.ppermute(value, axis, [(i, i ^ 1 << distance) for i in range(lax.axis...  7.41 us
    pallas_call x1, Pallas kernels, body(): pl.pallas_call(functools.partial(finish_kernel, hs, low), grid=grid, out_...  6.49 us
    unnamed x1, local copies, waits for them, and re-layouts  2.29 us
  transfers between devices with their start and end apart: 3, of which 3 were waited for; matrix products, arithmetic and copies ran while one was open for 0% of the time, Pallas kernels for 9%

profile of v1, /device:TPU:0, one launch (start us, length us, event | category | flops | bytes accessed | tf_op | source)
XLA Modules:
  0.0 113.8 jit_solution(15121397120309174407)
XLA Ops:
  0.0 18.7 %summary.1 = (bf16[2,8,128,128]{3,2,1,0:T(8,128)(2,1)}, bf16[8,3,256,256]{3,2,1,0:T(8,128)(2,1)}, bf16[512,1024]{1,0:T(8,128)(2,1)}) custom-call(s32[8]{0:T(128)} %doc_ref.3, bf16[512,1024]{1,0:T(8,128)(2,1)} %k_ref.3, bf16[512,1024]{1,0:T(8,128)(2,1)} %v_ref.3, f32[8,512]{1,0:T(8,128)} %log_ref.3, f32[8,512]{1,0:T(8,128)} %beta_ref.3), custom_call_target="tpu_custom_call" | custom-call | tf_op jit(solution)/shard_map/summary/pallas_call | solution.py:403
  18.7 2.9 %collective-permute-start = (bf16[2,8,128,128]{3,2,1,0:T(8,128)(2,1)}, bf16[2,8,128,128]{3,2,1,0:T(8,128)(2,1)S(1)}, u32[]{:S(2)}, u32[]{:S(2)}) collective-permute-start(bf16[2,8,128,128]{3,2,1,0:T(8,128)(2,1)} %get-tuple-element.14), channel_id=1, source_target_pairs={{0,4},{4,0},{8,12},{12,8},{16,20},{20,16},{24,28},{28,24},{1,5},{5... | collective-permute-start | bytes 1572872 | tf_op jit(solution)/shard_map/ppermute | solution.py:380
  21.6 12.1 %collective-permute-done = bf16[2,8,128,128]{3,2,1,0:T(8,128)(2,1)S(1)} collective-permute-done((bf16[2,8,128,128]{3,2,1,0:T(8,128)(2,1)}, bf16[2,8,128,128]{3,2,1,0:T(8,128)(2,1)S(1)}, u32[]{:S(2)}, u32[]{:S(2)}) %collective-permute-start) | collective-permute-done | bytes 524320 | tf_op jit(solution)/shard_map/ppermute | solution.py:380
  33.8 1.1 broadcast_select_fusion.3
  34.9 0.3 fusion.8
  35.2 0.1 fusion.23
  35.3 0.1 pad_maximum_fusion.1
  35.4 1.9 %collective-permute-start.1 = (bf16[2,8,128,128]{3,2,1,0:T(8,128)(2,1)S(1)}, bf16[2,8,128,128]{3,2,1,0:T(8,128)(2,1)S(1)}, u32[]{:S(2)}, u32[]{:S(2)}) collective-permute-start(bf16[2,8,128,128]{3,2,1,0:T(8,128)(2,1)S(1)} %pad_maximum_fusion.1), channel_id=1, source_target_pairs={{0,8},{4,12},{8,0},{12,4},{16,24},{20,28},{24,16},{28,20},{1,9},{5... | collective-permute-start | bytes 1572872 | tf_op jit(solution)/shard_map/ppermute | solution.py:380
  37.3 10.6 %local.1 = (f32[512,1024]{1,0:T(8,128)}, bf16[512,1024]{1,0:T(8,128)(2,1)}) custom-call(s32[8]{0:T(128)} %doc_ref.3, bf16[512,1024]{1,0:T(8,128)(2,1)} %q_ref.1, bf16[512,1024]{1,0:T(8,128)(2,1)} %k_ref.3, bf16[512,1024]{1,0:T(8,128)(2,1)} %v_ref.3, f32[8,512]{1,0:T(8,128)} %log_ref.3, f32[8,512]{1,0:T(8,128)} %beta_ref.3, f32[10,8,512]{2,1,0:T(8,128)} %w_ref.3, ...), custom_call_target="tpu_custom_call" | custom-call | flops 4000000000 | bytes 12000000 | tf_op jit(solution)/shard_map/local/pallas_call | solution.py:418
  47.9 0.1 fusion.7
  48.0 0.6 collective-permute-done.1
  48.6 0.1 broadcast_select_fusion.1
  48.7 0.3 fusion.16
  49.0 0.1 fusion.27
  49.1 0.1 pad_maximum_fusion.2
  49.2 2.6 %collective-permute-start.2 = (bf16[2,8,128,128]{3,2,1,0:T(8,128)(2,1)S(1)}, bf16[2,8,128,128]{3,2,1,0:T(8,128)(2,1)S(1)}, u32[]{:S(2)}, u32[]{:S(2)}) collective-permute-start(bf16[2,8,128,128]{3,2,1,0:T(8,128)(2,1)S(1)} %pad_maximum_fusion.2), channel_id=1, source_target_pairs={{0,16},{4,20},{8,24},{12,28},{16,0},{20,4},{24,8},{28,12},{1,17},{... | collective-permute-start | bytes 1572872 | tf_op jit(solution)/shard_map/ppermute | solution.py:380
  51.8 0.3 fusion.12
  52.1 0.1 fusion.24
  52.2 21.4 %collective-permute-done.2 = bf16[2,8,128,128]{3,2,1,0:T(8,128)(2,1)S(1)} collective-permute-done((bf16[2,8,128,128]{3,2,1,0:T(8,128)(2,1)S(1)}, bf16[2,8,128,128]{3,2,1,0:T(8,128)(2,1)S(1)}, u32[]{:S(2)}, u32[]{:S(2)}) %collective-permute-start.2) | collective-permute-done | bytes 524320 | tf_op jit(solution)/shard_map/ppermute | solution.py:380
  73.6 0.2 fusion.1
  73.9 1.0 pad_maximum_fusion.state_ref
  74.8 6.5 %finish.1.z_ref = bf16[512,1024]{1,0:T(8,128)(2,1)} custom-call(f32[512,1024]{1,0:T(8,128)} %get-tuple-element.12.y_ref, bf16[512,1024]{1,0:T(8,128)(2,1)} %get-tuple-element.13.reader_ref, bf16[3,8,128,128]{3,2,1,0:T(8,128)(2,1)} %pad_maximum_fusion.state_ref, f32[10,8,512]{2,1,0:T(8,128)} %w_ref.3, f32[1,1024]{1,0:T(1,128)} %bitcast.55), custom_call_target="tpu_custom_call" | custom-call | tf_op jit(solution)/shard_map/finish/pallas_call | solution.py:460
  81.3 30.2 %project.1 = bf16[128,4096]{1,0:T(8,128)(2,1)} custom-call(bf16[512,1024]{1,0:T(8,128)(2,1)} %finish.1.z_ref, bf16[1024,4096]{1,0:T(8,128)(2,1)} %w_hbm.1), custom_call_target="tpu_custom_call" | custom-call | tf_op jit(solution)/shard_map/project/pallas_call | solution.py:361
  111.5 2.3 %copy.11 = bf16[128,4096]{1,0:T(8,128)(2,1)} copy(bf16[128,4096]{1,0:T(8,128)(2,1)} %project.1) | data formatting | bytes 2097152
  (7 shorter events, 0.2 us)
Async XLA Ops:
  18.7 15.1 %collective-permute-start = (bf16[2,8,128,128]{3,2,1,0:T(8,128)(2,1)}, bf16[2,8,128,128]{3,2,1,0:T(8,128)(2,1)S(1)}, u32[]{:S(2)}, u32[]{:S(2)}) collective-permute-start(bf16[2,8,128,128]{3,2,1,0:T(8,128)(2,1)} %get-tuple-element.14), channel_id=1, source_target_pairs={{0,4},{4,0},{8,12},{12,8},{16,20},{20,16},{24,28},{28,24},{1,5},{5... | collective-permute-start | bytes 1572872 | tf_op jit(solution)/shard_map/ppermute | solution.py:380
  35.4 13.2 %collective-permute-start.1 = (bf16[2,8,128,128]{3,2,1,0:T(8,128)(2,1)S(1)}, bf16[2,8,128,128]{3,2,1,0:T(8,128)(2,1)S(1)}, u32[]{:S(2)}, u32[]{:S(2)}) collective-permute-start(bf16[2,8,128,128]{3,2,1,0:T(8,128)(2,1)S(1)} %pad_maximum_fusion.1), channel_id=1, source_target_pairs={{0,8},{4,12},{8,0},{12,4},{16,24},{20,28},{24,16},{28,20},{1,9},{5... | collective-permute-start | bytes 1572872 | tf_op jit(solution)/shard_map/ppermute | solution.py:380
  49.2 24.4 %collective-permute-start.2 = (bf16[2,8,128,128]{3,2,1,0:T(8,128)(2,1)S(1)}, bf16[2,8,128,128]{3,2,1,0:T(8,128)(2,1)S(1)}, u32[]{:S(2)}, u32[]{:S(2)}) collective-permute-start(bf16[2,8,128,128]{3,2,1,0:T(8,128)(2,1)S(1)} %pad_maximum_fusion.2), channel_id=1, source_target_pairs={{0,16},{4,20},{8,24},{12,28},{16,0},{20,4},{24,8},{28,12},{1,17},{... | collective-permute-start | bytes 1572872 | tf_op jit(solution)/shard_map/ppermute | solution.py:380

commit v2 on v1

--- a/solution.py
+++ b/solution.py
@@ -102,18 +102,9 @@
     return [inverse.astype(BF) for inverse in inverses]
 
 
-def summary_kernel(
-    heads_step, doc_ref, k_ref, v_ref, log_ref, beta_ref, map_ref, inv_ref, erase_ref, bias_ref, cum_ref
-):
+def form_maps(step, heads_step, doc_ref, k_ref, v_ref, beta_ref, inv_ref, erase_ref, map_ref, bias_ref, cum_ref):
     tokens = k_ref.shape[0]
     half = tokens // 2
-    step = pl.program_id(0)
-
-    @pl.when(step == 0)
-    def _():
-        fill_bias(doc_ref, bias_ref)
-        cum_ref[...] = prefix_sum(log_ref[...])
-
     ids_col = document_ids(doc_ref, (tokens, 1), 0)
     first_doc = ids_col == 0
     last_doc = ids_col == jnp.max(ids_col)
@@ -161,9 +152,9 @@
     for j in heads:
         c, key, cum, beta = col_of[j], keys[j], cums[j], betas[j]
         inv0, inv10, inv1 = inverses[2 * j], cross[j], inverses[2 * j + 1]
-        inv_ref[j, 0] = inv0
-        inv_ref[j, 1] = inv10
-        inv_ref[j, 2] = inv1
+        inv_ref[step, j, 0] = inv0
+        inv_ref[step, j, 1] = inv10
+        inv_ref[step, j, 2] = inv1
         gamma = jnp.where(first_doc, jnp.exp(cum), 0.0)
         tail = jnp.where(last_doc, jnp.exp(cum_rows[j][:, tokens - 1 : tokens] - cum), 0.0)
         rhs = jnp.concatenate(
@@ -172,26 +163,16 @@
         solved0 = mm(inv0, rhs[:half])
         solved1 = mm(inv10, rhs[:half]) + mm(inv1, rhs[half:])
         solved = jnp.concatenate([solved0, solved1], axis=0).astype(BF)
-        erase_ref[:, c] = solved[:, hd:]
+        erase_ref[step, :, c] = solved[:, hd:]
         out = mm_tn(tail * key, solved)
-        map_ref[0, j] = (gamma[tokens - 1 : tokens, :] * eye - out[:, hd:]).astype(BF)
-        map_ref[1, j] = out[:, :hd].astype(BF)
-
-
-def local_kernel(
-    heads_step, doc_ref, q_ref, k_ref, v_ref, log_ref, beta_ref, w_ref, inv_ref, erase_ref,
-    y_ref, reader_ref, bias_ref, cum_ref,
-):
+        map_ref[0, step, 0, j] = (gamma[tokens - 1 : tokens, :] * eye - out[:, hd:]).astype(BF)
+        map_ref[0, step, 1, j] = out[:, :hd].astype(BF)
+
+
+def read_block(step, heads_step, doc_ref, q_ref, k_ref, v_ref, beta_ref, w_ref, inv_ref, erase_ref, y_ref, reader_ref, bias_ref, cum_ref):
     tokens = k_ref.shape[0]
     half = tokens // 2
     quarter = half // 2
-    step = pl.program_id(0)
-
-    @pl.when(step == 0)
-    def _():
-        fill_bias(doc_ref, bias_ref)
-        cum_ref[...] = prefix_sum(log_ref[...])
-
     first = document_ids(doc_ref, (tokens, 1), 0) == 0
     hd = 128
     rows = lax.broadcasted_iota(jnp.int32, (quarter, quarter), 0)
@@ -230,34 +211,202 @@
             return jnp.concatenate([top, jnp.concatenate([b, c], axis=1)], axis=0)
 
         s00, s10, s11 = scores(0, 0), scores(1, 0), scores(1, 1)
-        inv0, inv10, inv1 = inv_ref[j, 0], inv_ref[j, 1], inv_ref[j, 2]
+        inv0, inv10, inv1 = inv_ref[step, j, 0], inv_ref[step, j, 1], inv_ref[step, j, 2]
         r00 = within(mm(s00, inv0), 0)
         r11 = within(mm(s11, inv1), 1)
         r10 = (mm(s10, inv0) + mm(s11, inv10)) * weights[3][half:]
         value = (beta * v_ref[:, cols].astype(F32)).astype(BF)
-        y_ref[:half, cols] = mm(r00, value[:half])
-        y_ref[half:, cols] = mm(r10, value[:half]) + mm(r11, value[half:])
-        erase = erase_ref[:, cols]
-        reader_ref[:half, cols] = (gamma[:half] * query[:half] - mm(s00, erase[:half])).astype(BF)
-        reader_ref[half:, cols] = (
+        y_ref[step, :half, cols] = mm(r00, value[:half])
+        y_ref[step, half:, cols] = mm(r10, value[:half]) + mm(r11, value[half:])
+        erase = erase_ref[step, :, cols]
+        reader_ref[step, :half, cols] = (gamma[:half] * query[:half] - mm(s00, erase[:half])).astype(BF)
+        reader_ref[step, half:, cols] = (
             gamma[half:] * query[half:] - mm(s10, erase[:half]) - mm(s11, erase[half:])
         ).astype(BF)
 
 
-def finish_kernel(heads_step, low, y_ref, reader_ref, state_ref, w_ref, gain_ref, z_ref):
-    step = pl.program_id(0)
+def finish_block(step, heads_step, low, y_ref, reader_ref, state_ref, w_ref, gain_ref, z_ref):
     hd = 128
     levels = state_ref.shape[0]
     for j in range(heads_step):
         h = step * heads_step + j
         cols = slice(j * hd, (j + 1) * hd)
         side = columns_of([w_ref[low + l, pl.ds(h, 1), :] for l in range(levels)])
-        y = y_ref[:, cols]
-        reader = reader_ref[:, cols]
+        y = y_ref[step, :, cols]
+        reader = reader_ref[step, :, cols]
         for l in range(levels):
-            y = y + side[:, l : l + 1] * mm(reader, state_ref[l, j])
+            y = y + side[:, l : l + 1] * mm(reader, state_ref[l, step, j])
         y = y * lax.rsqrt(jnp.mean(y * y, axis=-1, keepdims=True) + EPS)
         z_ref[:, cols] = (y * gain_ref[:, cols]).astype(BF)
+
+
+def mixer_kernel(
+    hs, low, doc_ref, q_ref, k_ref, v_ref, log_ref, beta_ref, w_ref, gain_ref, z_ref,
+    bias_ref, cum_ref, inv_ref, erase_ref, y_ref, reader_ref, send, recv, carried, states,
+    send_sem, recv_sem,
+):
+    step = pl.program_id(0)
+    nbits, groups = send.shape[0], send.shape[1]
+    hd = send.shape[-1]
+    block = lax.axis_index("seq")
+    barrier = pltpu.get_barrier_semaphore()
+
+    def partner(bit):
+        return block + (1 << bit) * (1 - 2 * ((block // (1 << bit)) % 2))
+
+    def copy(bit, g):
+        whole = bit < nbits - 1
+        return pltpu.make_async_remote_copy(
+            src_ref=send.at[bit, g] if whole else send.at[bit, g, 1],
+            dst_ref=recv.at[bit, g] if whole else recv.at[bit, g, 1],
+            send_sem=send_sem.at[bit, g],
+            recv_sem=recv_sem.at[bit, g],
+            device_id={"seq": partner(bit)},
+            device_id_type=pl.DeviceIdType.MESH,
+        )
+
+    @pl.when(step == 0)
+    def _():
+        for bit in range(nbits):
+            pl.semaphore_signal(
+                barrier, inc=1, device_id={"seq": partner(bit)}, device_id_type=pl.DeviceIdType.MESH
+            )
+        fill_bias(doc_ref, bias_ref)
+        cum_ref[...] = prefix_sum(log_ref[...])
+
+    @pl.when(step < groups)
+    def _():
+        form_maps(
+            step, hs, doc_ref, k_ref, v_ref, beta_ref, inv_ref, erase_ref, send, bias_ref, cum_ref
+        )
+
+    @pl.when(step == 0)
+    def _():
+        pl.semaphore_wait(barrier, nbits)
+
+    @pl.when(step < groups)
+    def _():
+        copy(0, step).start()
+
+    @pl.when((step >= groups) & (step < 2 * groups))
+    def _():
+        read_block(
+            step - groups, hs, doc_ref, q_ref, k_ref, v_ref, beta_ref, w_ref, inv_ref, erase_ref,
+            y_ref, reader_ref, bias_ref, cum_ref,
+        )
+
+    @pl.when(step >= 2 * groups)
+    def _():
+        finish_block(
+            step - 2 * groups, hs, low, y_ref, reader_ref, states, w_ref, gain_ref, z_ref
+        )
+
+    def exchange(bit, g):
+        copy(bit, g).wait_recv()
+        upper = (block // (1 << bit)) % 2 == 1
+        eye = jnp.where(
+            lax.broadcasted_iota(jnp.int32, (hd, hd), 0)
+            == lax.broadcasted_iota(jnp.int32, (hd, hd), 1),
+            1.0,
+            0.0,
+        )
+        more = bit < nbits - 1
+        for j in range(hs):
+            sib_s = recv[bit, g, 1, j]
+            if more:
+                sib_t = recv[bit, g, 0, j]
+            if bit == 0:
+                reached_s = sib_s.astype(F32)
+                if more:
+                    carried[g, j] = jnp.where(upper, sib_t.astype(F32), eye)
+            elif more:
+                held = carried[g, j]
+                both = mm(held, jnp.concatenate([sib_t, sib_s], axis=1))
+                reached_s = both[:, hd:]
+                carried[g, j] = jnp.where(upper, both[:, :hd], held)
+            else:
+                reached_s = mm(carried[g, j], sib_s)
+            states[bit, g, j] = jnp.where(upper, reached_s, 0.0).astype(BF)
+            if more:
+                sib = jnp.concatenate([sib_t, sib_s], axis=1).astype(F32)
+                own = jnp.concatenate([send[bit, g, 0, j], send[bit, g, 1, j]], axis=1).astype(F32)
+                first = jnp.where(upper, sib, own)
+                second = jnp.where(upper, own, sib)
+                merged = mm(second[:, :hd], first)
+                send[bit + 1, g, 0, j] = merged[:, :hd].astype(BF)
+                send[bit + 1, g, 1, j] = (merged[:, hd:] + second[:, hd:]).astype(BF)
+        if more:
+            copy(bit + 1, g).start()
+
+    for bit in range(nbits):
+        g = step - 1 - bit
+
+        @pl.when((g >= 0) & (g < groups))
+        def _(bit=bit, g=g):
+            exchange(bit, g)
+
+    @pl.when(step == 3 * groups - 1)
+    def _():
+        for bit in range(nbits):
+            for g in range(groups):
+                copy(bit, g).wait_send()
+
+
+def mixer(queries, keys, values, log_decay, beta, level_weights, doc_start, norm_gain):
+    tokens = queries.shape[0]
+    heads = log_decay.shape[0]
+    hd = queries.shape[1] // heads
+    half = tokens // 2
+    hs = 2
+    groups = heads // hs
+    low = (tokens // SPAN).bit_length()
+    nbits = lax.axis_size("seq").bit_length() - 1
+    wide = (tokens, hs * hd)
+
+    def both(i):
+        return (0, jnp.minimum(i, 2 * groups - 1) % groups)
+
+    def second(i):
+        return (0, jnp.clip(i - groups, 0, groups - 1))
+
+    def third(i):
+        return (0, jnp.clip(i - 2 * groups, 0, groups - 1))
+
+    row_block = pl.BlockSpec((heads, tokens), lambda i: (0, 0))
+    return pl.pallas_call(
+        functools.partial(mixer_kernel, hs, low),
+        grid=(3 * groups,),
+        out_shape=jax.ShapeDtypeStruct((tokens, heads * hd), BF),
+        in_specs=[
+            pl.BlockSpec(memory_space=pltpu.SMEM),
+            pl.BlockSpec(wide, second),
+            pl.BlockSpec(wide, both),
+            pl.BlockSpec(wide, both),
+            row_block,
+            row_block,
+            pl.BlockSpec(level_weights.shape, lambda i: (0, 0, 0)),
+            pl.BlockSpec((1, hs * hd), third),
+        ],
+        out_specs=pl.BlockSpec(wide, third),
+        scratch_shapes=[
+            pltpu.VMEM((tokens, tokens), F32),
+            pltpu.VMEM((heads, tokens), F32),
+            pltpu.VMEM((groups, hs, 3, half, half), BF),
+            pltpu.VMEM((groups, tokens, hs * hd), BF),
+            pltpu.VMEM((groups, tokens, hs * hd), F32),
+            pltpu.VMEM((groups, tokens, hs * hd), BF),
+            pltpu.VMEM((nbits, groups, 2, hs, hd, hd), BF),
+            pltpu.VMEM((nbits, groups, 2, hs, hd, hd), BF),
+            pltpu.VMEM((groups, hs, hd, hd), F32),
+            pltpu.VMEM((nbits, groups, hs, hd, hd), BF),
+            pltpu.SemaphoreType.DMA((nbits, groups)),
+            pltpu.SemaphoreType.DMA((nbits, groups)),
+        ],
+        compiler_params=pltpu.CompilerParams(
+            collective_id=1, has_side_effects=True, vmem_limit_bytes=56 * 2**20
+        ),
+        name="mixer",
+    )(doc_start, queries, keys, values, log_decay, beta, level_weights, norm_gain.reshape(1, -1))
 
 
 def project_kernel(
@@ -376,102 +525,10 @@
     )(normed, out_weight)
 
 
-def from_partner(value, axis, distance):
-    return lax.ppermute(value, axis, [(i, i ^ 1 << distance) for i in range(lax.axis_size(axis))])
-
-
-def bmm(a, b):
-    return jnp.einsum("hde,hef->hdf", a, b, preferred_element_type=F32)
-
-
 def body(queries, keys, values, log_decay, beta, level_weights, doc_start, norm_gain, out_weight):
-    tokens = queries.shape[0]
-    heads = log_decay.shape[0]
-    hd = queries.shape[1] // heads
-    half = tokens // 2
-    hs = 2
-    low = (tokens // SPAN).bit_length()
-    grid = (heads // hs,)
-    smem = pl.BlockSpec(memory_space=pltpu.SMEM)
-    wide = pl.BlockSpec((tokens, hs * hd), lambda i: (0, i))
-    whole = pl.BlockSpec((heads, tokens), lambda i: (0, 0))
-    level_block = pl.BlockSpec(level_weights.shape, lambda i: (0, 0, 0))
-    inv_block = pl.BlockSpec((hs, 3, half, half), lambda i: (i, 0, 0, 0))
-    map_block = pl.BlockSpec((2, hs, hd, hd), lambda i: (0, i, 0, 0))
-    params = pltpu.CompilerParams(vmem_limit_bytes=56 * 2**20)
-    scratch = [pltpu.VMEM((tokens, tokens), F32), pltpu.VMEM((heads, tokens), F32)]
-    maps, inv, erase = pl.pallas_call(
-        functools.partial(summary_kernel, hs),
-        grid=grid,
-        out_shape=(
-            jax.ShapeDtypeStruct((2, heads, hd, hd), BF),
-            jax.ShapeDtypeStruct((heads, 3, half, half), BF),
-            jax.ShapeDtypeStruct((tokens, heads * hd), BF),
-        ),
-        in_specs=[smem, wide, wide, whole, whole],
-        out_specs=(map_block, inv_block, wide),
-        scratch_shapes=scratch,
-        compiler_params=params,
-        name="summary",
-    )(doc_start, keys, values, log_decay, beta)
-
-    y_local, reader = pl.pallas_call(
-        functools.partial(local_kernel, hs),
-        grid=grid,
-        out_shape=(
-            jax.ShapeDtypeStruct((tokens, heads * hd), F32),
-            jax.ShapeDtypeStruct((tokens, heads * hd), BF),
-        ),
-        in_specs=[smem, wide, wide, wide, whole, whole, level_block, inv_block, wide],
-        out_specs=(wide, wide),
-        scratch_shapes=scratch,
-        compiler_params=params,
-        cost_estimate=pl.CostEstimate(flops=4 * 10**9, bytes_accessed=12 * 10**6, transcendentals=0),
-        name="local",
-    )(doc_start, queries, keys, values, log_decay, beta, level_weights, inv, erase)
-
-    nbits = lax.axis_size("seq").bit_length() - 1
-    block_idx = lax.axis_index("seq")
-    current = maps
-    carried = None
-    states = []
-    for bit in range(nbits):
-        sibling = from_partner(current, "seq", bit)
-        upper = block_idx >> bit & 1 == 1
-        if carried is None:
-            reached = sibling.astype(F32)
-        else:
-            both = jnp.concatenate([sibling[0], sibling[1]], axis=-1)
-            reached = bmm(carried.astype(BF), both)
-            reached = jnp.stack([reached[..., :hd], reached[..., hd:]])
-        states.append(jnp.where(upper, reached[1], 0.0).astype(BF))
-        if bit < nbits - 1:
-            idle = jnp.broadcast_to(jnp.eye(hd, dtype=F32), (heads, hd, hd)) if bit == 0 else carried
-            carried = jnp.where(upper, reached[0], idle)
-            first = jnp.where(upper, sibling, current)
-            second = jnp.where(upper, current, sibling)
-            both = jnp.concatenate([first[0], first[1]], axis=-1)
-            merged = bmm(second[0], both)
-            current = jnp.stack(
-                [merged[..., :hd], merged[..., hd:] + second[1].astype(F32)]
-            ).astype(BF)
-    states = jnp.stack(states)
-
-    normed = pl.pallas_call(
-        functools.partial(finish_kernel, hs, low),
-        grid=grid,
-        out_shape=jax.ShapeDtypeStruct((tokens, heads * hd), BF),
-        in_specs=[
-            wide,
-            wide,
-            pl.BlockSpec((nbits, hs, hd, hd), lambda i: (0, i, 0, 0)),
-            level_block,
-            pl.BlockSpec((1, hs * hd), lambda i: (0, i)),
-        ],
-        out_specs=wide,
-        compiler_params=params,
-        name="finish",
-    )(y_local, reader, states, level_weights, norm_gain.reshape(1, -1))
+    normed = mixer(
+        queries, keys, values, log_decay, beta, level_weights, doc_start, norm_gain
+    )
     return project(normed, out_weight)
 
 

time: 114 us -> 77 us (0.68)
  waiting for transfers between devices: 34.1 us -> 0 us
  Pallas kernels: 66 us -> 74.4 us
  starting transfers between devices: 7.41 us -> 0 us
  other arithmetic: 2.52 us -> 0 us
    ppermute x3 -> x0, waiting for transfers between devices: 34.1 us -> none  [from_partner(): lax.ppermute(value, axis, [(i, i ^ 1 << distance) for i in range(lax.axis...]
    pallas_call x3 -> x1, Pallas kernels: 35.8 us -> 43.8 us  [mixer(): pl.pallas_call(functools.partial(mixer_kernel, hs, low), grid=(3 * groups...]
    ppermute x3 -> x0, starting transfers between devices: 7.41 us -> none  [from_partner(): lax.ppermute(value, axis, [(i, i ^ 1 << distance) for i in range(lax.axis...]
    another operation x6 -> x0, other arithmetic: 1.27 us -> none  [the longest x2 1.02 us: body(): states = jnp.stack(states)]
    select_n x2 -> x0, other arithmetic: 1.19 us -> none  [body(): second = jnp.where(upper, current, sibling)]
  transfers between devices with their start and end apart: 3 -> 0, of which waited for: 3 -> 0; matrix products, arithmetic and copies ran while one was open for 0% -> 0% of each run, Pallas kernels for 9% -> 0%
where the time goes in v2:
time: 77 us; the launch traced here: 76.8 us
  Pallas kernels  74.4 us (97%)
  local copies, waits for them, and re-layouts  2.29 us (3%)
    pallas_call x1, Pallas kernels, mixer(): pl.pallas_call(functools.partial(mixer_kernel, hs, low), grid=(3 * groups...  43.8 us
    pallas_call x1, Pallas kernels, project(): pl.pallas_call(functools.partial(project_kernel, chunk), out_shape=jax.Sh...  30.6 us
    unnamed x1, local copies, waits for them, and re-layouts  2.29 us

profile of v2, /device:TPU:0, one launch (start us, length us, event | category | flops | bytes accessed | tf_op | source)
XLA Modules:
  0.0 76.8 jit_solution(6036524934946519556)
XLA Ops:
  0.0 43.8 %mixer.1.z_ref = bf16[512,1024]{1,0:T(8,128)(2,1)} custom-call(s32[8]{0:T(128)} %doc_ref.1, bf16[512,1024]{1,0:T(8,128)(2,1)} %q_ref.1, bf16[512,1024]{1,0:T(8,128)(2,1)} %k_ref.1, bf16[512,1024]{1,0:T(8,128)(2,1)} %v_ref.1, f32[8,512]{1,0:T(8,128)} %log_ref.1, f32[8,512]{1,0:T(8,128)} %beta_ref.1, f32[10,8,512]{2,1,0:T(8,128)} %w_ref.1, f32[1,1024]{1,0:T(1,128)} %bitcast.1), custom_call_target="tpu_custom_call" | custom-call | tf_op jit(solution)/shard_map/mixer/pallas_call | solution.py:376
  43.9 30.6 %project.1 = bf16[128,4096]{1,0:T(8,128)(2,1)} custom-call(bf16[512,1024]{1,0:T(8,128)(2,1)} %mixer.1.z_ref, bf16[1024,4096]{1,0:T(8,128)(2,1)} %w_hbm.1), custom_call_target="tpu_custom_call" | custom-call | tf_op jit(solution)/shard_map/project/pallas_call | solution.py:510
  74.5 2.3 %copy.11 = bf16[128,4096]{1,0:T(8,128)(2,1)} copy(bf16[128,4096]{1,0:T(8,128)(2,1)} %project.1) | data formatting | bytes 2097152

commit v3 on v2

--- a/solution.py
+++ b/solution.py
@@ -225,30 +225,124 @@
         ).astype(BF)
 
 
-def finish_block(step, heads_step, low, y_ref, reader_ref, state_ref, w_ref, gain_ref, z_ref):
+def finish_rows(half_idx, hs, low, y_ref, reader_ref, state_ref, w_ref, gain_ref, z_ref):
     hd = 128
     levels = state_ref.shape[0]
-    for j in range(heads_step):
-        h = step * heads_step + j
-        cols = slice(j * hd, (j + 1) * hd)
-        side = columns_of([w_ref[low + l, pl.ds(h, 1), :] for l in range(levels)])
-        y = y_ref[step, :, cols]
-        reader = reader_ref[step, :, cols]
-        for l in range(levels):
-            y = y + side[:, l : l + 1] * mm(reader, state_ref[l, step, j])
-        y = y * lax.rsqrt(jnp.mean(y * y, axis=-1, keepdims=True) + EPS)
-        z_ref[:, cols] = (y * gain_ref[:, cols]).astype(BF)
-
-
-def mixer_kernel(
-    hs, low, doc_ref, q_ref, k_ref, v_ref, log_ref, beta_ref, w_ref, gain_ref, z_ref,
+    half = z_ref.shape[0] // 2
+    part = pl.ds(pl.multiple_of(half_idx * half, half), half)
+
+    def group(g, _):
+        for j in range(hs):
+            h = g * hs + j
+            cols = slice(j * hd, (j + 1) * hd)
+            out_cols = pl.ds(pl.multiple_of(h * hd, hd), hd)
+            side = columns_of([w_ref[low + l, pl.ds(h, 1), part] for l in range(levels)])
+            y = y_ref[g, part, cols]
+            reader = reader_ref[g, part, cols]
+            for l in range(levels):
+                y = y + side[:, l : l + 1] * mm(reader, state_ref[l, g, j])
+            y = y * lax.rsqrt(jnp.mean(y * y, axis=-1, keepdims=True) + EPS)
+            z_ref[part, out_cols] = (y * gain_ref[:, out_cols]).astype(BF)
+        return 0
+
+    lax.fori_loop(0, state_ref.shape[1], group, 0)
+
+
+def project_rows(me, finish, weight_load, z_ref, w_ref, out_ref, keep, slabs, sems):
+    mate = me + 1 - 2 * (me % 2)
+    across = (me + 2) % 4
+    send_a, recv_a, send_y, recv_y, send_b, recv_b = slabs
+    sa_sem, ra_sem, sy_sem, ry_sem, sb_sem, rb_sem = sems
+    count, rows, chunk = keep.shape[1:]
+    near = me // 2
+    far = 1 - near
+
+    def columns(j):
+        return pl.ds(pl.multiple_of(j * chunk, chunk), chunk)
+
+    def remote(src, dst, ssem, rsem, j, target):
+        return pltpu.make_async_remote_copy(
+            src_ref=src.at[j],
+            dst_ref=dst.at[j],
+            send_sem=ssem.at[j],
+            recv_sem=rsem.at[j],
+            device_id={"head": target},
+            device_id_type=pl.DeviceIdType.MESH,
+        )
+
+    def copy_a(j):
+        return remote(send_a, recv_a, sa_sem, ra_sem, j, mate)
+
+    def copy_b(j):
+        return remote(send_b, recv_b, sb_sem, rb_sem, j, mate)
+
+    def copy_y(j):
+        return remote(send_y, recv_y, sy_sem, ry_sem, j, across)
+
+    def terms(half_idx, j):
+        part = pl.ds(pl.multiple_of(half_idx * 2 * rows, 2 * rows), 2 * rows)
+        product = jnp.dot(z_ref[part, :], w_ref[:, columns(j)], preferred_element_type=F32)
+        first = me % 2 == 0
+        top, bottom = product[:rows], product[rows:]
+        return jnp.where(first, top, bottom), jnp.where(first, bottom, top)
+
+    def forward(j):
+        copy_a(j).wait_recv()
+        send_y[j] = (keep[0, j] + recv_a[j].astype(F32)).astype(BF)
+        copy_y(j).start()
+
+    def far_step(j, _):
+        weight_load(j).wait()
+        mine, other = terms(far, j)
+        send_a[j] = other.astype(BF)
+        copy_a(j).start()
+        keep[0, j] = mine
+
+        @pl.when(j > 0)
+        def _():
+            forward(j - 1)
+
+        return 0
+
+    def near_step(j, _):
+        mine, other = terms(near, j)
+        send_b[j] = other.astype(BF)
+        copy_b(j).start()
+        keep[1, j] = mine
+        return 0
+
+    def close(j, _):
+        copy_b(j).wait_recv()
+        copy_y(j).wait_recv()
+        total = keep[1, j] + recv_b[j].astype(F32) + recv_y[j].astype(F32)
+        out_ref[:, columns(j)] = total.astype(BF)
+        copy_a(j).wait_send()
+        copy_b(j).wait_send()
+        copy_y(j).wait_send()
+        return 0
+
+    finish(far)
+    lax.fori_loop(0, count, far_step, 0)
+    forward(count - 1)
+    finish(near)
+    lax.fori_loop(0, count, near_step, 0)
+    lax.fori_loop(0, count, close, 0)
+
+
+def layer_kernel(
+    hs, low, doc_ref, q_ref, k_ref, v_ref, log_ref, beta_ref, w_ref, gain_ref, weight_hbm, out_ref,
     bias_ref, cum_ref, inv_ref, erase_ref, y_ref, reader_ref, send, recv, carried, states,
-    send_sem, recv_sem,
+    z_ref, weight_ref, keep, send_a, recv_a, send_y, recv_y, send_b, recv_b,
+    send_sem, recv_sem, load_sem, sa_sem, ra_sem, sy_sem, ry_sem, sb_sem, rb_sem,
 ):
     step = pl.program_id(0)
     nbits, groups = send.shape[0], send.shape[1]
     hd = send.shape[-1]
     block = lax.axis_index("seq")
+    me = lax.axis_index("head")
+    mate = me + 1 - 2 * (me % 2)
+    across = (me + 2) % 4
+    count, chunk = keep.shape[1], keep.shape[3]
     barrier = pltpu.get_barrier_semaphore()
 
     def partner(bit):
@@ -265,14 +359,23 @@
             device_id_type=pl.DeviceIdType.MESH,
         )
 
+    def weight_load(j):
+        cols = pl.ds(pl.multiple_of(j * chunk, chunk), chunk)
+        return pltpu.make_async_copy(weight_hbm.at[:, cols], weight_ref.at[:, cols], load_sem.at[j])
+
     @pl.when(step == 0)
     def _():
+        for other in (mate, across):
+            pl.semaphore_signal(
+                barrier, inc=1, device_id={"head": other}, device_id_type=pl.DeviceIdType.MESH
+            )
         for bit in range(nbits):
             pl.semaphore_signal(
                 barrier, inc=1, device_id={"seq": partner(bit)}, device_id_type=pl.DeviceIdType.MESH
             )
         fill_bias(doc_ref, bias_ref)
         cum_ref[...] = prefix_sum(log_ref[...])
+        lax.fori_loop(0, count, lambda j, _: (weight_load(j).start(), 0)[1], 0)
 
     @pl.when(step < groups)
     def _():
@@ -282,7 +385,7 @@
 
     @pl.when(step == 0)
     def _():
-        pl.semaphore_wait(barrier, nbits)
+        pl.semaphore_wait(barrier, nbits + 2)
 
     @pl.when(step < groups)
     def _():
@@ -293,12 +396,6 @@
         read_block(
             step - groups, hs, doc_ref, q_ref, k_ref, v_ref, beta_ref, w_ref, inv_ref, erase_ref,
             y_ref, reader_ref, bias_ref, cum_ref,
-        )
-
-    @pl.when(step >= 2 * groups)
-    def _():
-        finish_block(
-            step - 2 * groups, hs, low, y_ref, reader_ref, states, w_ref, gain_ref, z_ref
         )
 
     def exchange(bit, g):
@@ -341,18 +438,37 @@
     for bit in range(nbits):
         g = step - 1 - bit
 
-        @pl.when((g >= 0) & (g < groups))
+        @pl.when((step < 2 * groups) & (g >= 0) & (g < groups))
         def _(bit=bit, g=g):
             exchange(bit, g)
 
-    @pl.when(step == 3 * groups - 1)
+    @pl.when(step == 2 * groups)
     def _():
+        for late in range(2 * groups, groups + nbits):
+            for bit in range(nbits):
+                if 0 <= late - 1 - bit < groups:
+                    exchange(bit, late - 1 - bit)
+
+        def finish(half_idx):
+            finish_rows(half_idx, hs, low, y_ref, reader_ref, states, w_ref, gain_ref, z_ref)
+
+        project_rows(
+            me,
+            finish,
+            weight_load,
+            z_ref,
+            weight_ref,
+            out_ref,
+            keep,
+            (send_a, recv_a, send_y, recv_y, send_b, recv_b),
+            (sa_sem, ra_sem, sy_sem, ry_sem, sb_sem, rb_sem),
+        )
         for bit in range(nbits):
             for g in range(groups):
                 copy(bit, g).wait_send()
 
 
-def mixer(queries, keys, values, log_decay, beta, level_weights, doc_start, norm_gain):
+def body(queries, keys, values, log_decay, beta, level_weights, doc_start, norm_gain, out_weight):
     tokens = queries.shape[0]
     heads = log_decay.shape[0]
     hd = queries.shape[1] // heads
@@ -362,6 +478,10 @@
     low = (tokens // SPAN).bit_length()
     nbits = lax.axis_size("seq").bit_length() - 1
     wide = (tokens, hs * hd)
+    rows = tokens // lax.axis_size("head")
+    out_width = out_weight.shape[1]
+    chunk = min(512, out_width)
+    count = out_width // chunk
 
     def both(i):
         return (0, jnp.minimum(i, 2 * groups - 1) % groups)
@@ -369,14 +489,11 @@
     def second(i):
         return (0, jnp.clip(i - groups, 0, groups - 1))
 
-    def third(i):
-        return (0, jnp.clip(i - 2 * groups, 0, groups - 1))
-
     row_block = pl.BlockSpec((heads, tokens), lambda i: (0, 0))
     return pl.pallas_call(
-        functools.partial(mixer_kernel, hs, low),
-        grid=(3 * groups,),
-        out_shape=jax.ShapeDtypeStruct((tokens, heads * hd), BF),
+        functools.partial(layer_kernel, hs, low),
+        grid=(2 * groups + 1,),
+        out_shape=jax.ShapeDtypeStruct((rows, out_width), BF),
         in_specs=[
             pl.BlockSpec(memory_space=pltpu.SMEM),
             pl.BlockSpec(wide, second),
@@ -385,9 +502,10 @@
             row_block,
             row_block,
             pl.BlockSpec(level_weights.shape, lambda i: (0, 0, 0)),
-            pl.BlockSpec((1, hs * hd), third),
+            pl.BlockSpec((1, heads * hd), lambda i: (0, 0)),
+            pl.BlockSpec(memory_space=pl.ANY),
         ],
-        out_specs=pl.BlockSpec(wide, third),
+        out_specs=pl.BlockSpec((rows, out_width), lambda i: (0, 0)),
         scratch_shapes=[
             pltpu.VMEM((tokens, tokens), F32),
             pltpu.VMEM((heads, tokens), F32),
@@ -399,137 +517,21 @@
             pltpu.VMEM((nbits, groups, 2, hs, hd, hd), BF),
             pltpu.VMEM((groups, hs, hd, hd), F32),
             pltpu.VMEM((nbits, groups, hs, hd, hd), BF),
-            pltpu.SemaphoreType.DMA((nbits, groups)),
-            pltpu.SemaphoreType.DMA((nbits, groups)),
-        ],
-        compiler_params=pltpu.CompilerParams(
-            collective_id=1, has_side_effects=True, vmem_limit_bytes=56 * 2**20
-        ),
-        name="mixer",
-    )(doc_start, queries, keys, values, log_decay, beta, level_weights, norm_gain.reshape(1, -1))
-
-
-def project_kernel(
-    chunk, z_ref, w_hbm, out_ref, w_ref, keep, send_a, recv_a, send_y, recv_y, send_b, recv_b,
-    w_sem, sa_sem, ra_sem, sy_sem, ry_sem, sb_sem, rb_sem,
-):
-    me = lax.axis_index("head")
-    mate = me + 1 - 2 * (me % 2)
-    across = (me + 2) % 4
-    far_mate = (mate + 2) % 4
-    count = keep.shape[1]
-    rows = keep.shape[2]
-
-    def columns(j):
-        return pl.ds(pl.multiple_of(j * chunk, chunk), chunk)
-
-    def load(j):
-        return pltpu.make_async_copy(w_hbm.at[:, columns(j)], w_ref.at[:, columns(j)], w_sem.at[j])
-
-    def remote(src, dst, ssem, rsem, j, target):
-        return pltpu.make_async_remote_copy(
-            src_ref=src.at[j],
-            dst_ref=dst.at[j],
-            send_sem=ssem.at[j],
-            recv_sem=rsem.at[j],
-            device_id={"head": target},
-            device_id_type=pl.DeviceIdType.MESH,
-        )
-
-    def copy_a(j):
-        return remote(send_a, recv_a, sa_sem, ra_sem, j, mate)
-
-    def copy_b(j):
-        return remote(send_b, recv_b, sb_sem, rb_sem, j, mate)
-
-    def copy_y(j):
-        return remote(send_y, recv_y, sy_sem, ry_sem, j, across)
-
-    def block(owner):
-        return z_ref[pl.ds(pl.multiple_of(owner * rows, rows), rows), :]
-
-    lax.fori_loop(0, count, lambda j, _: (load(j).start(), 0)[1], 0)
-    barrier = pltpu.get_barrier_semaphore()
-    for other in (mate, across):
-        pl.semaphore_signal(
-            barrier, inc=1, device_id={"head": other}, device_id_type=pl.DeviceIdType.MESH
-        )
-    pl.semaphore_wait(barrier, 2)
-
-    def forward(j):
-        copy_a(j).wait_recv()
-        send_y[j] = (keep[0, j] + recv_a[j].astype(F32)).astype(BF)
-        copy_y(j).start()
-
-    def far(j, _):
-        load(j).wait()
-        weight = w_ref[:, columns(j)]
-        send_a[j] = jnp.dot(block(far_mate), weight, preferred_element_type=F32).astype(BF)
-        copy_a(j).start()
-        keep[0, j] = jnp.dot(block(across), weight, preferred_element_type=F32)
-
-        @pl.when(j > 0)
-        def _():
-            forward(j - 1)
-
-        return 0
-
-    lax.fori_loop(0, count, far, 0)
-    forward(count - 1)
-
-    def near(j, _):
-        weight = w_ref[:, columns(j)]
-        send_b[j] = jnp.dot(block(mate), weight, preferred_element_type=F32).astype(BF)
-        copy_b(j).start()
-        keep[1, j] = jnp.dot(block(me), weight, preferred_element_type=F32)
-        return 0
-
-    lax.fori_loop(0, count, near, 0)
-
-    def close(j, _):
-        copy_b(j).wait_recv()
-        copy_y(j).wait_recv()
-        total = keep[1, j] + recv_b[j].astype(F32) + recv_y[j].astype(F32)
-        out_ref[:, columns(j)] = total.astype(BF)
-        copy_a(j).wait_send()
-        copy_b(j).wait_send()
-        copy_y(j).wait_send()
-        return 0
-
-    lax.fori_loop(0, count, close, 0)
-
-
-def project(normed, out_weight):
-    tokens, width = normed.shape
-    out_width = out_weight.shape[1]
-    rows = tokens // 4
-    chunk = min(512, out_width)
-    count = out_width // chunk
-    slab = pltpu.VMEM((count, rows, chunk), BF)
-    sems = [pltpu.SemaphoreType.DMA((count,))] * 7
-    return pl.pallas_call(
-        functools.partial(project_kernel, chunk),
-        out_shape=jax.ShapeDtypeStruct((rows, out_width), BF),
-        in_specs=[pl.BlockSpec(memory_space=pltpu.VMEM), pl.BlockSpec(memory_space=pl.ANY)],
-        out_specs=pl.BlockSpec(memory_space=pltpu.VMEM),
-        scratch_shapes=[
-            pltpu.VMEM((width, out_width), BF),
+            pltpu.VMEM((tokens, heads * hd), BF),
+            pltpu.VMEM(out_weight.shape, BF),
             pltpu.VMEM((2, count, rows, chunk), F32),
         ]
-        + [slab] * 6
-        + sems,
+        + [pltpu.VMEM((count, rows, chunk), BF)] * 6
+        + [pltpu.SemaphoreType.DMA((nbits, groups))] * 2
+        + [pltpu.SemaphoreType.DMA((count,))] * 7,
         compiler_params=pltpu.CompilerParams(
             collective_id=0, has_side_effects=True, vmem_limit_bytes=56 * 2**20
         ),
-        name="project",
-    )(normed, out_weight)
-
-
-def body(queries, keys, values, log_decay, beta, level_weights, doc_start, norm_gain, out_weight):
-    normed = mixer(
-        queries, keys, values, log_decay, beta, level_weights, doc_start, norm_gain
+        name="layer",
+    )(
+        doc_start, queries, keys, values, log_decay, beta, level_weights,
+        norm_gain.reshape(1, -1), out_weight,
     )
-    return project(normed, out_weight)
 
 
 def solution(mesh):

time: 77 us -> 71.9 us (0.934)
  Pallas kernels: 74.4 us -> 69.5 us
    pallas_call x2 -> x1, Pallas kernels: 74.4 us -> 69.5 us  [body(): pl.pallas_call(functools.partial(layer_kernel, hs, low), grid=(2 * groups...]
where the time goes in v3:
time: 71.9 us; the launch traced here: 71.7 us
  Pallas kernels  69.5 us (97%)
  local copies, waits for them, and re-layouts  2.29 us (3%)
    pallas_call x1, Pallas kernels, body(): pl.pallas_call(functools.partial(layer_kernel, hs, low), grid=(2 * groups...  69.5 us
    unnamed x1, local copies, waits for them, and re-layouts  2.29 us

profile of v3, /device:TPU:0, one launch (start us, length us, event | category | flops | bytes accessed | tf_op | source)
XLA Modules:
  0.0 71.7 jit_solution(3742790459906502821)
XLA Ops:
  0.0 69.5 %layer.1 = bf16[128,4096]{1,0:T(8,128)(2,1)} custom-call(s32[8]{0:T(128)} %doc_ref.1, bf16[512,1024]{1,0:T(8,128)(2,1)} %q_ref.1, bf16[512,1024]{1,0:T(8,128)(2,1)} %k_ref.1, bf16[512,1024]{1,0:T(8,128)(2,1)} %v_ref.1, f32[8,512]{1,0:T(8,128)} %log_ref.1, f32[8,512]{1,0:T(8,128)} %beta_ref.1, f32[10,8,512]{2,1,0:T(8,128)} %w_ref.1, f32[1,1024]{1,0:T(1,128)} %bitcast.1, ...), custom_call_target="tpu_custom_call" | custom-call | tf_op jit(solution)/shard_map/layer/pallas_call | solution.py:493
  69.5 2.3 %copy.11 = bf16[128,4096]{1,0:T(8,128)(2,1)} copy(bf16[128,4096]{1,0:T(8,128)(2,1)} %layer.1) | data formatting | bytes 2097152

commit v4 on v3

--- a/solution.py
+++ b/solution.py
@@ -68,35 +68,49 @@
     return jnp.concatenate(rows, axis=0).T
 
 
-def unit_lower_inverses(lowers):
-    size = lowers[0].shape[0]
-    rows = lax.broadcasted_iota(jnp.int32, (size, size), 0)
-    cols = lax.broadcasted_iota(jnp.int32, (size, size), 1)
-    apart = rows ^ cols
+def pair_diagonal(pair):
+    size = pair.shape[0]
+    pair = pair.astype(BF)
+    zero = jnp.zeros((size, size), BF)
+    top = jnp.concatenate([pair[:, :size], zero], axis=1)
+    return jnp.concatenate([top, jnp.concatenate([zero, pair[:, size:]], axis=1)], axis=0)
+
+
+def unit_lower_inverses(pairs):
+    size = pairs[0].shape[0]
+    rows = lax.broadcasted_iota(jnp.int32, (size, 2 * size), 0)
+    cols = lax.broadcasted_iota(jnp.int32, (size, 2 * size), 1)
+    apart = rows ^ (cols % size)
     eye = jnp.where(apart == 0, 1.0, 0.0)
     base = 16
     inside = (apart < base) & (apart > 0)
-    powers = [jnp.where(inside, lower, 0.0) for lower in lowers]
+    powers = [jnp.where(inside, pair, 0.0) for pair in pairs]
     inverses = [eye - power for power in powers]
-    powers = [mm(power, power) for power in powers]
+    powers = [mm(power, pair_diagonal(power)) for power in powers]
     reach = 2
     while reach < base:
         if 2 * reach < base:
             both = [
-                mm(jnp.concatenate([power.astype(BF), inverse.astype(BF)], axis=0), power)
+                mm(
+                    jnp.concatenate([power.astype(BF), inverse.astype(BF)], axis=0),
+                    pair_diagonal(power),
+                )
                 for power, inverse in zip(powers, inverses)
             ]
-            powers = [pair[:size] for pair in both]
-            inverses = [inverse + pair[size:] for inverse, pair in zip(inverses, both)]
+            powers = [item[:size] for item in both]
+            inverses = [inverse + item[size:] for inverse, item in zip(inverses, both)]
         else:
-            inverses = [inverse + mm(inverse, power) for power, inverse in zip(powers, inverses)]
+            inverses = [
+                inverse + mm(inverse, pair_diagonal(power))
+                for power, inverse in zip(powers, inverses)
+            ]
         reach *= 2
     while base < size:
         band = (apart >= base) & (apart < 2 * base)
-        offs = [jnp.where(band, lower, 0.0).astype(BF) for lower in lowers]
+        offs = [pair_diagonal(jnp.where(band, pair, 0.0)) for pair in pairs]
         held = [inverse.astype(BF) for inverse in inverses]
         steps = [mm(inverse, off) for inverse, off in zip(held, offs)]
-        steps = [mm(first, inverse) for first, inverse in zip(steps, held)]
+        steps = [mm(first, pair_diagonal(inverse)) for first, inverse in zip(steps, held)]
         inverses = [inverse - step for inverse, step in zip(inverses, steps)]
         base *= 2
     return [inverse.astype(BF) for inverse in inverses]
@@ -131,8 +145,14 @@
         return ratio * mm_nt(keys_b[j][rs], keys_b[j][cs]) * betas[j][rs]
 
     piece = [slice(i * quarter, (i + 1) * quarter) for i in range(parts)]
-    diagonal = unit_lower_inverses([lower(j, p, p) for j in heads for p in piece])
     merges = [(j, i) for j in heads for i in range(0, parts, 2)]
+    paired = unit_lower_inverses(
+        [
+            jnp.concatenate([lower(j, piece[i + k], piece[i + k]) for k in range(2)], axis=1)
+            for j, i in merges
+        ]
+    )
+    diagonal = [pair[:, k * quarter : (k + 1) * quarter] for pair in paired for k in range(2)]
     firsts = [
         mm(diagonal[j * parts + i + 1], lower(j, piece[i + 1], piece[i])) for j, i in merges
     ]
@@ -169,7 +189,7 @@
         map_ref[0, step, 1, j] = out[:, :hd].astype(BF)
 
 
-def read_block(step, heads_step, doc_ref, q_ref, k_ref, v_ref, beta_ref, w_ref, inv_ref, erase_ref, y_ref, reader_ref, bias_ref, cum_ref):
+def read_half(which, step, heads_step, doc_ref, q_ref, k_ref, v_ref, beta_ref, w_ref, inv_ref, erase_ref, y_ref, reader_ref, bias_ref, cum_ref):
     tokens = k_ref.shape[0]
     half = tokens // 2
     quarter = half // 2
@@ -210,45 +230,46 @@
             top = jnp.concatenate([a, jnp.zeros_like(a)], axis=1)
             return jnp.concatenate([top, jnp.concatenate([b, c], axis=1)], axis=0)
 
-        s00, s10, s11 = scores(0, 0), scores(1, 0), scores(1, 1)
         inv0, inv10, inv1 = inv_ref[step, j, 0], inv_ref[step, j, 1], inv_ref[step, j, 2]
-        r00 = within(mm(s00, inv0), 0)
+        value = (beta * v_ref[:, cols].astype(F32)).astype(BF)
+        erase = erase_ref[step, :, cols]
+        if which == 0:
+            s00 = scores(0, 0)
+            r00 = within(mm(s00, inv0), 0)
+            y_ref[step, :half, cols] = mm(r00, value[:half])
+            reader_ref[step, :half, cols] = (
+                gamma[:half] * query[:half] - mm(s00, erase[:half])
+            ).astype(BF)
+            continue
+        s10, s11 = scores(1, 0), scores(1, 1)
         r11 = within(mm(s11, inv1), 1)
         r10 = (mm(s10, inv0) + mm(s11, inv10)) * weights[3][half:]
-        value = (beta * v_ref[:, cols].astype(F32)).astype(BF)
-        y_ref[step, :half, cols] = mm(r00, value[:half])
         y_ref[step, half:, cols] = mm(r10, value[:half]) + mm(r11, value[half:])
-        erase = erase_ref[step, :, cols]
-        reader_ref[step, :half, cols] = (gamma[:half] * query[:half] - mm(s00, erase[:half])).astype(BF)
         reader_ref[step, half:, cols] = (
             gamma[half:] * query[half:] - mm(s10, erase[:half]) - mm(s11, erase[half:])
         ).astype(BF)
 
 
-def finish_rows(half_idx, hs, low, y_ref, reader_ref, state_ref, w_ref, gain_ref, z_ref):
+def finish_rows(half_idx, g, hs, low, y_ref, reader_ref, state_ref, w_ref, gain_ref, z_ref):
     hd = 128
     levels = state_ref.shape[0]
     half = z_ref.shape[0] // 2
     part = pl.ds(pl.multiple_of(half_idx * half, half), half)
 
-    def group(g, _):
-        for j in range(hs):
-            h = g * hs + j
-            cols = slice(j * hd, (j + 1) * hd)
-            out_cols = pl.ds(pl.multiple_of(h * hd, hd), hd)
-            side = columns_of([w_ref[low + l, pl.ds(h, 1), part] for l in range(levels)])
-            y = y_ref[g, part, cols]
-            reader = reader_ref[g, part, cols]
-            for l in range(levels):
-                y = y + side[:, l : l + 1] * mm(reader, state_ref[l, g, j])
-            y = y * lax.rsqrt(jnp.mean(y * y, axis=-1, keepdims=True) + EPS)
-            z_ref[part, out_cols] = (y * gain_ref[:, out_cols]).astype(BF)
-        return 0
-
-    lax.fori_loop(0, state_ref.shape[1], group, 0)
-
-
-def project_rows(me, finish, weight_load, z_ref, w_ref, out_ref, keep, slabs, sems):
+    for j in range(hs):
+        h = g * hs + j
+        cols = slice(j * hd, (j + 1) * hd)
+        out_cols = pl.ds(pl.multiple_of(h * hd, hd), hd)
+        side = columns_of([w_ref[low + l, pl.ds(h, 1), part] for l in range(levels)])
+        y = y_ref[g, part, cols]
+        reader = reader_ref[g, part, cols]
+        for l in range(levels):
+            y = y + side[:, l : l + 1] * mm(reader, state_ref[l, g, j])
+        y = y * lax.rsqrt(jnp.mean(y * y, axis=-1, keepdims=True) + EPS)
+        z_ref[part, out_cols] = (y * gain_ref[:, out_cols]).astype(BF)
+
+
+def project_rows(me, finish_far, finish_near, weight_load, z_ref, w_ref, out_ref, keep, slabs, sems):
     mate = me + 1 - 2 * (me % 2)
     across = (me + 2) % 4
     send_a, recv_a, send_y, recv_y, send_b, recv_b = slabs
@@ -321,12 +342,33 @@
         copy_y(j).wait_send()
         return 0
 
-    finish(far)
+    finish_far(far)
     lax.fori_loop(0, count, far_step, 0)
     forward(count - 1)
-    finish(near)
+    finish_near(near)
     lax.fori_loop(0, count, near_step, 0)
     lax.fori_loop(0, count, close, 0)
+
+
+def exchange_slots(nbits, groups):
+    form, first, second, hop = 4.6, 0.9, 1.7, 3.5
+    times = [(form * (at + 1), (at, 1)) for at in range(groups)]
+    now = form * groups
+    for at in range(groups, 2 * groups):
+        times += [(now + first, (at, 0)), (now + first + second, (at, 1))]
+        now += first + second
+    slots, late = {}, []
+    for g in range(groups):
+        sent = form * (g + 1)
+        for bit in range(nbits):
+            open_slots = [(t, key) for t, key in times if sent is not None and t >= sent + hop]
+            if open_slots:
+                sent, key = open_slots[0]
+                slots.setdefault(key, []).append((bit, g))
+            else:
+                sent = None
+                late.append((bit, g))
+    return slots, late
 
 
 def layer_kernel(
@@ -386,17 +428,6 @@
     @pl.when(step == 0)
     def _():
         pl.semaphore_wait(barrier, nbits + 2)
-
-    @pl.when(step < groups)
-    def _():
-        copy(0, step).start()
-
-    @pl.when((step >= groups) & (step < 2 * groups))
-    def _():
-        read_block(
-            step - groups, hs, doc_ref, q_ref, k_ref, v_ref, beta_ref, w_ref, inv_ref, erase_ref,
-            y_ref, reader_ref, bias_ref, cum_ref,
-        )
 
     def exchange(bit, g):
         copy(bit, g).wait_recv()
@@ -435,26 +466,57 @@
         if more:
             copy(bit + 1, g).start()
 
-    for bit in range(nbits):
-        g = step - 1 - bit
-
-        @pl.when((step < 2 * groups) & (g >= 0) & (g < groups))
-        def _(bit=bit, g=g):
+    slots, late = exchange_slots(nbits, groups)
+
+    def run_slot(at, part):
+        for bit, g in slots.get((at, part), ()):
             exchange(bit, g)
+
+    for at in range(groups):
+
+        @pl.when(step == at)
+        def _(at=at):
+            copy(0, at).start()
+            run_slot(at, 1)
+
+    def read(which):
+        read_half(
+            which, step - groups, hs, doc_ref, q_ref, k_ref, v_ref, beta_ref, w_ref, inv_ref,
+            erase_ref, y_ref, reader_ref, bias_ref, cum_ref,
+        )
+
+    for part in range(2):
+
+        @pl.when((step >= groups) & (step < 2 * groups))
+        def _(part=part):
+            read(part)
+
+        for at in range(groups, 2 * groups):
+            if (at, part) in slots:
+
+                @pl.when(step == at)
+                def _(at=at, part=part):
+                    run_slot(at, part)
 
     @pl.when(step == 2 * groups)
     def _():
-        for late in range(2 * groups, groups + nbits):
-            for bit in range(nbits):
-                if 0 <= late - 1 - bit < groups:
-                    exchange(bit, late - 1 - bit)
-
-        def finish(half_idx):
-            finish_rows(half_idx, hs, low, y_ref, reader_ref, states, w_ref, gain_ref, z_ref)
+        def finish(half_idx, g):
+            finish_rows(half_idx, g, hs, low, y_ref, reader_ref, states, w_ref, gain_ref, z_ref)
+
+        def finish_far(half_idx):
+            for g in range(groups):
+                for bit, owner in late:
+                    if owner == g:
+                        exchange(bit, owner)
+                finish(half_idx, g)
+
+        def finish_near(half_idx):
+            lax.fori_loop(0, groups, lambda g, _: (finish(half_idx, g), 0)[1], 0)
 
         project_rows(
             me,
-            finish,
+            finish_far,
+            finish_near,
             weight_load,
             z_ref,
             weight_ref,

time: 71.9 us -> 69.8 us (0.971)
  Pallas kernels: 69.5 us -> 67.3 us
    pallas_call x1, Pallas kernels: 69.5 us -> 67.3 us  [body(): pl.pallas_call(functools.partial(layer_kernel, hs, low), grid=(2 * groups...]
where the time goes in v4:
time: 69.8 us; the launch traced here: 69.6 us
  Pallas kernels  67.3 us (96%)
  local copies, waits for them, and re-layouts  2.29 us (3%)
    pallas_call x1, Pallas kernels, body(): pl.pallas_call(functools.partial(layer_kernel, hs, low), grid=(2 * groups...  67.3 us
    unnamed x1, local copies, waits for them, and re-layouts  2.29 us

profile of v4, /device:TPU:0, one launch (start us, length us, event | category | flops | bytes accessed | tf_op | source)
XLA Modules:
  0.0 69.6 jit_solution(12959504312514175874)
XLA Ops:
  0.0 67.3 %layer.1 = bf16[128,4096]{1,0:T(8,128)(2,1)} custom-call(s32[8]{0:T(128)} %doc_ref.1, bf16[512,1024]{1,0:T(8,128)(2,1)} %q_ref.1, bf16[512,1024]{1,0:T(8,128)(2,1)} %k_ref.1, bf16[512,1024]{1,0:T(8,128)(2,1)} %v_ref.1, f32[8,512]{1,0:T(8,128)} %log_ref.1, f32[8,512]{1,0:T(8,128)} %beta_ref.1, f32[10,8,512]{2,1,0:T(8,128)} %w_ref.1, f32[1,1024]{1,0:T(1,128)} %bitcast.1, ...), custom_call_target="tpu_custom_call" | custom-call | tf_op jit(solution)/shard_map/layer/pallas_call | solution.py:555
  67.4 2.3 %copy.11 = bf16[128,4096]{1,0:T(8,128)(2,1)} copy(bf16[128,4096]{1,0:T(8,128)(2,1)} %layer.1) | data formatting | bytes 2097152

commit v5 on v4

--- a/solution.py
+++ b/solution.py
@@ -269,7 +269,7 @@
         z_ref[part, out_cols] = (y * gain_ref[:, out_cols]).astype(BF)
 
 
-def project_rows(me, finish_far, finish_near, weight_load, z_ref, w_ref, out_ref, keep, slabs, sems):
+def project_rows(is_far, me, weight_load, z_ref, w_ref, out_ref, keep, slabs, sems):
     mate = me + 1 - 2 * (me % 2)
     across = (me + 2) % 4
     send_a, recv_a, send_y, recv_y, send_b, recv_b = slabs
@@ -342,21 +342,21 @@
         copy_y(j).wait_send()
         return 0
 
-    finish_far(far)
-    lax.fori_loop(0, count, far_step, 0)
-    forward(count - 1)
-    finish_near(near)
-    lax.fori_loop(0, count, near_step, 0)
-    lax.fori_loop(0, count, close, 0)
+    if is_far:
+        lax.fori_loop(0, count, far_step, 0)
+        forward(count - 1)
+    else:
+        lax.fori_loop(0, count, near_step, 0)
+        lax.fori_loop(0, count, close, 0)
 
 
 def exchange_slots(nbits, groups):
-    form, first, second, hop = 4.6, 0.9, 1.7, 3.5
+    form, read, hop = 4.4, 1.75, 3.4
     times = [(form * (at + 1), (at, 1)) for at in range(groups)]
     now = form * groups
     for at in range(groups, 2 * groups):
-        times += [(now + first, (at, 0)), (now + first + second, (at, 1))]
-        now += first + second
+        now += read
+        times.append((now, (at, 1)))
     slots, late = {}, []
     for g in range(groups):
         sent = form * (g + 1)
@@ -479,44 +479,36 @@
             copy(0, at).start()
             run_slot(at, 1)
 
-    def read(which):
-        read_half(
-            which, step - groups, hs, doc_ref, q_ref, k_ref, v_ref, beta_ref, w_ref, inv_ref,
-            erase_ref, y_ref, reader_ref, bias_ref, cum_ref,
-        )
-
-    for part in range(2):
-
-        @pl.when((step >= groups) & (step < 2 * groups))
-        def _(part=part):
-            read(part)
-
-        for at in range(groups, 2 * groups):
-            if (at, part) in slots:
-
-                @pl.when(step == at)
-                def _(at=at, part=part):
-                    run_slot(at, part)
-
-    @pl.when(step == 2 * groups)
-    def _():
-        def finish(half_idx, g):
-            finish_rows(half_idx, g, hs, low, y_ref, reader_ref, states, w_ref, gain_ref, z_ref)
-
-        def finish_far(half_idx):
-            for g in range(groups):
-                for bit, owner in late:
-                    if owner == g:
-                        exchange(bit, owner)
-                finish(half_idx, g)
-
-        def finish_near(half_idx):
-            lax.fori_loop(0, groups, lambda g, _: (finish(half_idx, g), 0)[1], 0)
-
+    far = 1 - me // 2
+    near_start = 2 * groups + 1
+    before = step < 2 * groups
+    half_now = jnp.where(before, far, 1 - far)
+    group_now = jnp.where(before, step - groups, step - near_start)
+    reading = (step >= groups) & (step != 2 * groups) & (step < near_start + groups)
+
+    for which in range(2):
+
+        @pl.when(reading & (half_now == which))
+        def _(which=which):
+            read_half(
+                which, group_now, hs, doc_ref, q_ref, k_ref, v_ref, beta_ref, w_ref, inv_ref,
+                erase_ref, y_ref, reader_ref, bias_ref, cum_ref,
+            )
+
+    for at in range(groups, 2 * groups):
+        if (at, 1) in slots:
+
+            @pl.when(step == at)
+            def _(at=at):
+                run_slot(at, 1)
+
+    def finish(half_idx, g):
+        finish_rows(half_idx, g, hs, low, y_ref, reader_ref, states, w_ref, gain_ref, z_ref)
+
+    def project(is_far):
         project_rows(
+            is_far,
             me,
-            finish_far,
-            finish_near,
             weight_load,
             z_ref,
             weight_ref,
@@ -525,6 +517,23 @@
             (send_a, recv_a, send_y, recv_y, send_b, recv_b),
             (sa_sem, ra_sem, sy_sem, ry_sem, sb_sem, rb_sem),
         )
+
+    @pl.when(step == 2 * groups)
+    def _():
+        for g in range(groups):
+            for bit, owner in late:
+                if owner == g:
+                    exchange(bit, owner)
+            finish(far, g)
+        project(True)
+
+    @pl.when((step >= near_start) & (step < near_start + groups))
+    def _():
+        finish(1 - far, group_now)
+
+    @pl.when(step == near_start + groups)
+    def _():
+        project(False)
         for bit in range(nbits):
             for g in range(groups):
                 copy(bit, g).wait_send()
@@ -546,15 +555,16 @@
     count = out_width // chunk
 
     def both(i):
-        return (0, jnp.minimum(i, 2 * groups - 1) % groups)
+        return (0, jnp.where(i < 2 * groups, i % groups, jnp.clip(i - 2 * groups - 1, 0, groups - 1)))
 
     def second(i):
-        return (0, jnp.clip(i - groups, 0, groups - 1))
+        late = jnp.clip(i - 2 * groups - 1, 0, groups - 1)
+        return (0, jnp.where(i < 2 * groups, jnp.clip(i - groups, 0, groups - 1), late))
 
     row_block = pl.BlockSpec((heads, tokens), lambda i: (0, 0))
     return pl.pallas_call(
         functools.partial(layer_kernel, hs, low),
-        grid=(2 * groups + 1,),
+        grid=(3 * groups + 2,),
         out_shape=jax.ShapeDtypeStruct((rows, out_width), BF),
         in_specs=[
             pl.BlockSpec(memory_space=pltpu.SMEM),

time: 69.8 us -> 68.3 us (0.979)
  Pallas kernels: 67.3 us -> 65.7 us
    pallas_call x1, Pallas kernels: 67.3 us -> 65.7 us  [body(): pl.pallas_call(functools.partial(layer_kernel, hs, low), grid=(3 * groups...]
where the time goes in v5:
time: 68.3 us; the launch traced here: 68 us
  Pallas kernels  65.7 us (96%)
  local copies, waits for them, and re-layouts  2.29 us (3%)
    pallas_call x1, Pallas kernels, body(): pl.pallas_call(functools.partial(layer_kernel, hs, low), grid=(3 * groups...  65.7 us
    unnamed x1, local copies, waits for them, and re-layouts  2.29 us

profile of v5, /device:TPU:0, one launch (start us, length us, event | category | flops | bytes accessed | tf_op | source)
XLA Modules:
  0.0 68.0 jit_solution(6624493189007906392)
XLA Ops:
  0.0 65.7 %layer.1 = bf16[128,4096]{1,0:T(8,128)(2,1)} custom-call(s32[8]{0:T(128)} %doc_ref.1, bf16[512,1024]{1,0:T(8,128)(2,1)} %q_ref.1, bf16[512,1024]{1,0:T(8,128)(2,1)} %k_ref.1, bf16[512,1024]{1,0:T(8,128)(2,1)} %v_ref.1, f32[8,512]{1,0:T(8,128)} %log_ref.1, f32[8,512]{1,0:T(8,128)} %beta_ref.1, f32[10,8,512]{2,1,0:T(8,128)} %w_ref.1, f32[1,1024]{1,0:T(1,128)} %bitcast.1, ...), custom_call_target="tpu_custom_call" | custom-call | tf_op jit(solution)/shard_map/layer/pallas_call | solution.py:565
  65.7 2.3 %copy.11 = bf16[128,4096]{1,0:T(8,128)(2,1)} copy(bf16[128,4096]{1,0:T(8,128)(2,1)} %layer.1) | data formatting | bytes 2097152
